TPU v7x, 128 devices: a whole 4x4x4 slice. The times are simulated.
128 devices in a mesh: grp: 2 (over y_hi), dev: 64 (over z, x, y_lo, core).
Axes of the slice: x: 4, y: 4 (y_hi: 2, y_lo: 2; y = y_hi * 2 + y_lo), z: 4, core: 2. Of those that a mesh axis runs over, the one named last changes fastest.
Arguments:
- positions: float32 [3, 393216], P(None, ('grp', 'dev')), may hold values from -1 to 1
- strengths: float32 [3, 393216], P(None, ('grp', 'dev')), may hold values from -0.75 to 0.75
- plan: int32 [8, 128], P(None, ('grp', 'dev')), may hold values from 0 to 127, as said below
Outputs:
- velocity: float32 [3, 393216], P(None, ('grp', 'dev'))
- new_strengths: float32 [3, 393216], P(None, ('grp', 'dev'))
Inputs may be any that keep to these rules, and one draw needn't show every extreme that they name: In round r every block b is paired with plan[r, b] = b XOR m_r, where m_r is the same for all blocks and has exactly two set bits, and the m_r of the 8 rounds are distinct; so each round pairs the blocks two by two and no two blocks meet twice.
All inputs are finite; a program needn't handle non-finite values.
Results may differ from a plain program's by a relative error of at most 0.0003.
Values sent between devices are 32-bit elements; how exact they have to be, the bound alone decides.
No kernel may reach another device: no remote copies, remote signals or barrier semaphores. Data moves between devices by JAX's collectives and lax.ppermute only.
A program may use at most 64 MiB of HBM per device.

v0:
```python
import math

import jax
import jax.numpy as jnp
from jax import lax
from jax.sharding import PartitionSpec as P

SMOOTH_SQ = 0.01
INV_FOUR_PI = 1.0 / (4.0 * math.pi)
STEP_RATE = 0.25


def partner(shard, axis, stride):
    return lax.ppermute(shard, axis, [(i, i ^ 1 << stride) for i in range(lax.axis_size(axis))])


def cross_lists(first, second):
    return [
        first[1] * second[2] - first[2] * second[1],
        first[2] * second[0] - first[0] * second[2],
        first[0] * second[1] - first[1] * second[0],
    ]


def pair_terms(targets, sources):
    offsets = [targets[component][:, None] - sources[component][None, :] for component in range(3)]
    dist_sq = (
        offsets[0] * offsets[0] + offsets[1] * offsets[1] + offsets[2] * offsets[2] + SMOOTH_SQ
    )
    inverse = lax.rsqrt(dist_sq)
    cube = inverse * inverse * inverse
    fifth = 3.0 * cube * inverse * inverse
    source_str = [sources[3 + component][None, :] for component in range(3)]
    target_str = [targets[3 + component][:, None] for component in range(3)]
    swirl = cross_lists(offsets, source_str)
    spin = cross_lists(target_str, source_str)
    along = target_str[0] * offsets[0] + target_str[1] * offsets[1] + target_str[2] * offsets[2]
    target_rows = [jnp.sum(cube * swirl[component], 1) for component in range(3)]
    target_rows = target_rows + [
        jnp.sum(cube * spin[component] - fifth * along * swirl[component], 1)
        for component in range(3)
    ]
    back_swirl = cross_lists(target_str, offsets)
    source_along = (
        source_str[0] * offsets[0] + source_str[1] * offsets[1] + source_str[2] * offsets[2]
    )
    source_rows = [jnp.sum(cube * back_swirl[component], 0) for component in range(3)]
    source_rows = source_rows + [
        jnp.sum(fifth * source_along * back_swirl[component] - cube * spin[component], 0)
        for component in range(3)
    ]
    return (-INV_FOUR_PI * jnp.stack(target_rows), -INV_FOUR_PI * jnp.stack(source_rows))


def one_side(targets, sources):
    return pair_terms(targets, sources)[0]


def blocked(targets, sources):
    count = targets.shape[1]
    rows = min(1024, count)
    pieces = targets.reshape(6, count // rows, rows).transpose(1, 0, 2)
    result = lax.map(lambda piece: one_side(piece, sources), pieces)
    return result.transpose(1, 0, 2).reshape(6, count)


def half_terms(own_half, visit_half):
    return pair_terms(own_half, visit_half)


def split_terms(own, visitor, lower):
    count = own.shape[1]
    half_len = count // 2
    arranged = jnp.where(lower, visitor, jnp.roll(visitor, half_len, axis=1))
    own_halves = own.reshape(6, 2, half_len).transpose(1, 0, 2)
    visit_halves = arranged.reshape(6, 2, half_len).transpose(1, 0, 2)
    own_part, visit_part = lax.map(
        lambda pieces: half_terms(pieces[0], pieces[1]), (own_halves, visit_halves)
    )
    own_part = own_part.transpose(1, 0, 2).reshape(6, count)
    visit_part = visit_part.transpose(1, 0, 2).reshape(6, count)
    visit_part = jnp.where(lower, visit_part, jnp.roll(visit_part, half_len, axis=1))
    return (own_part, visit_part)


def route_block(state, offset_mask, levels):
    for bit_number in range(levels):
        flag = jnp.bitwise_and(jnp.right_shift(offset_mask, bit_number), 1) == 1
        state = lax.cond(
            flag, lambda held: partner(held, ("grp", "dev"), bit_number), lambda held: held, state
        )
    return state


def body(positions, strengths, plan):
    levels = lax.axis_size(("grp", "dev")).bit_length() - 1
    own_index = lax.axis_index(("grp", "dev"))
    partners = plan[:, 0]
    round_masks = jnp.bitwise_xor(partners, own_index)
    rounds = plan.shape[0]
    home = jnp.concatenate([positions, strengths], 0)
    totals = blocked(home, home)

    def home_round(round_no, running):
        offset_mask = round_masks[round_no]
        visitor = route_block(home, offset_mask, levels)
        own_part, visit_part = split_terms(home, visitor, own_index < partners[round_no])
        return running + own_part + route_block(visit_part, offset_mask, levels)

    totals = lax.fori_loop(0, rounds, home_round, totals)
    velocity = totals[:3]
    stretch = totals[3:]
    local_peak = jnp.max(jnp.sum(stretch * stretch, 0))
    peak_sq = lax.pmax(local_peak, ("grp", "dev"))
    new_strengths = strengths + STEP_RATE / (jnp.sqrt(peak_sq) + 1e-06) * stretch
    return (velocity, new_strengths)


def solution(mesh):
    placed = (P(None, ("grp", "dev")), P(None, ("grp", "dev")), P(None, ("grp", "dev")))
    return jax.shard_map(
        body,
        mesh=mesh,
        in_specs=placed,
        out_specs=(P(None, ("grp", "dev")), P(None, ("grp", "dev"))),
        check_vma=False,
    )
```

profile of v0, /device:TPU:1, one launch (start us, length us, event | category | flops | bytes accessed | tf_op | source)
XLA Modules:
  0.0 948.3 jit_solution(10515589846213511331)
XLA Ops:
  2.2 99.3 %while.51 = (s32[]{:T(128)}, f32[3,6,1024]{2,1,0:T(8,128)S(1)}, f32[3,6,1024]{2,1,0:T(8,128)S(1)}, f32[3,3072]{1,0:T(4,128)S(1)}, f32[3,3072]{1,0:T(4,128)S(1)},...) while((s32[]{:T(128)}, f32[3,6,1024]{2,1,0:T(8,128)S(1)}, ...), condition=%wide.region_7.8_spmd, body=%wide.region_0.7_spmd.sunk | while | flops 176160768 | bytes 434381 | solution.py:63
  2.4 32.9 %fusion.81 = (f32[1024]{0:T(1024)S(1)}, f32[1024]{0:T(1024)S(1)}, f32[1024]{0:T(1024)S(1)}, f32[1024]{0:T(1024)S(1)}, f32[1024]{0:T(1024)S(1)}, /*index=5*/f32[1024]{0:T(1024)S(1)}) fusion(f32[1024]{0:T(1024)S(1)} %bitcast.132, f32[1024]{0:T(1024)S(1)} %bitcast.128, f32[3072]{0:T(1024)S(1)} %bitcast.116, f32[3072]{0:T(1024)S(1)} %bitcast.117, ...), kind=kLoop, calls=%fused_computation.28.clone.1 | loop fusion | flops 176154624 | bytes 122880 | tf_op jit(solution)/shard_map/while/body/eval_jaxpr/reduce_sum | solution.py:40
  35.4 32.9 %fusion.81 = (f32[1024]{0:T(1024)S(1)}, f32[1024]{0:T(1024)S(1)}, f32[1024]{0:T(1024)S(1)}, f32[1024]{0:T(1024)S(1)}, f32[1024]{0:T(1024)S(1)}, /*index=5*/f32[1024]{0:T(1024)S(1)}) fusion(f32[1024]{0:T(1024)S(1)} %bitcast.132, f32[1024]{0:T(1024)S(1)} %bitcast.128, f32[3072]{0:T(1024)S(1)} %bitcast.116, f32[3072]{0:T(1024)S(1)} %bitcast.117, ...), kind=kLoop, calls=%fused_computation.28.clone.1 | loop fusion | flops 176154624 | bytes 122880 | tf_op jit(solution)/shard_map/while/body/eval_jaxpr/reduce_sum | solution.py:40
  68.5 32.9 %fusion.81 = (f32[1024]{0:T(1024)S(1)}, f32[1024]{0:T(1024)S(1)}, f32[1024]{0:T(1024)S(1)}, f32[1024]{0:T(1024)S(1)}, f32[1024]{0:T(1024)S(1)}, /*index=5*/f32[1024]{0:T(1024)S(1)}) fusion(f32[1024]{0:T(1024)S(1)} %bitcast.132, f32[1024]{0:T(1024)S(1)} %bitcast.128, f32[3072]{0:T(1024)S(1)} %bitcast.116, f32[3072]{0:T(1024)S(1)} %bitcast.117, ...), kind=kLoop, calls=%fused_computation.28.clone.1 | loop fusion | flops 176154624 | bytes 122880 | tf_op jit(solution)/shard_map/while/body/eval_jaxpr/reduce_sum | solution.py:40
  101.5 769.0 %while.53 = (s32[]{:T(128)}, f32[6,3072]{1,0:T(8,128)S(1)}, f32[6,3072]{1,0:T(8,128)S(1)}, s32[8]{0:T(128)S(1)}, s32[]{:T(128)}, /*index=5*/s32[8]{0:T(128)S(1)}...) while((s32[]{:T(128)}, f32[6,3072]{1,0:T(8,128)S(1)}, ...), condition=%wide.region_51.52_spmd, body=%wide.region_8.51_spmd.sunk | while | flops 203010080 | bytes 7865823 | solution.py:110
  109.4 6.5 conditional.34
  119.0 69.0 %while.54 = (s32[]{:T(128)}, f32[2,6,1536]{2,1,0:T(8,128)S(1)}, f32[2,6,1536]{2,1,0:T(8,128)S(1)}, f32[2,6,1536]{2,1,0:T(8,128)S(1)}, f32[2,6,1536]{2,1,0:T(8,12...) while((s32[]{:T(128)}, f32[2,6,1536]{2,1,0:T(8,128)S(1)}, ...), condition=%wide.region_36.36_spmd, body=%wide.region_23.35_spmd.sunk | while | flops 202899456 | bytes 786661 | solution.py:77
  119.2 33.9 %fusion.84 = (f32[1536]{0:T(1024)S(1)}, f32[1536]{0:T(1024)S(1)}, f32[1536]{0:T(1024)S(1)}, f32[1536]{0:T(1024)S(1)}, f32[1536]{0:T(1024)S(1)}, /*index=5*/f32[1...) fusion(f32[1536]{0:T(1024)S(1)} %get-tuple-element.515, ...), kind=kLoop, calls=%fused_computation.94.clone.1 | loop fusion | flops 202881024 | bytes 147456 | tf_op jit(solution)/shard_map/while/body/eval_jaxpr/while/body/eval_jaxpr/reduce_sum | solution.py:49
  153.7 33.9 %fusion.84 = (f32[1536]{0:T(1024)S(1)}, f32[1536]{0:T(1024)S(1)}, f32[1536]{0:T(1024)S(1)}, f32[1536]{0:T(1024)S(1)}, f32[1536]{0:T(1024)S(1)}, /*index=5*/f32[1...) fusion(f32[1536]{0:T(1024)S(1)} %get-tuple-element.515, ...), kind=kLoop, calls=%fused_computation.94.clone.1 | loop fusion | flops 202881024 | bytes 147456 | tf_op jit(solution)/shard_map/while/body/eval_jaxpr/while/body/eval_jaxpr/reduce_sum | solution.py:49
  190.3 5.6 conditional.41
  200.9 5.0 conditional.30
  211.5 69.0 %while.54 = (s32[]{:T(128)}, f32[2,6,1536]{2,1,0:T(8,128)S(1)}, f32[2,6,1536]{2,1,0:T(8,128)S(1)}, f32[2,6,1536]{2,1,0:T(8,128)S(1)}, f32[2,6,1536]{2,1,0:T(8,12...) while((s32[]{:T(128)}, f32[2,6,1536]{2,1,0:T(8,128)S(1)}, ...), condition=%wide.region_36.36_spmd, body=%wide.region_23.35_spmd.sunk | while | flops 202899456 | bytes 786661 | solution.py:77
  211.7 33.9 %fusion.84 = (f32[1536]{0:T(1024)S(1)}, f32[1536]{0:T(1024)S(1)}, f32[1536]{0:T(1024)S(1)}, f32[1536]{0:T(1024)S(1)}, f32[1536]{0:T(1024)S(1)}, /*index=5*/f32[1...) fusion(f32[1536]{0:T(1024)S(1)} %get-tuple-element.515, ...), kind=kLoop, calls=%fused_computation.94.clone.1 | loop fusion | flops 202881024 | bytes 147456 | tf_op jit(solution)/shard_map/while/body/eval_jaxpr/while/body/eval_jaxpr/reduce_sum | solution.py:49
  246.2 33.9 %fusion.84 = (f32[1536]{0:T(1024)S(1)}, f32[1536]{0:T(1024)S(1)}, f32[1536]{0:T(1024)S(1)}, f32[1536]{0:T(1024)S(1)}, f32[1536]{0:T(1024)S(1)}, /*index=5*/f32[1...) fusion(f32[1536]{0:T(1024)S(1)} %get-tuple-element.515, ...), kind=kLoop, calls=%fused_computation.94.clone.1 | loop fusion | flops 202881024 | bytes 147456 | tf_op jit(solution)/shard_map/while/body/eval_jaxpr/while/body/eval_jaxpr/reduce_sum | solution.py:49
  295.8 4.6 conditional.32
  304.7 69.0 %while.54 = (s32[]{:T(128)}, f32[2,6,1536]{2,1,0:T(8,128)S(1)}, f32[2,6,1536]{2,1,0:T(8,128)S(1)}, f32[2,6,1536]{2,1,0:T(8,128)S(1)}, f32[2,6,1536]{2,1,0:T(8,12...) while((s32[]{:T(128)}, f32[2,6,1536]{2,1,0:T(8,128)S(1)}, ...), condition=%wide.region_36.36_spmd, body=%wide.region_23.35_spmd.sunk | while | flops 202899456 | bytes 786661 | solution.py:77
  305.0 33.9 %fusion.84 = (f32[1536]{0:T(1024)S(1)}, f32[1536]{0:T(1024)S(1)}, f32[1536]{0:T(1024)S(1)}, f32[1536]{0:T(1024)S(1)}, f32[1536]{0:T(1024)S(1)}, /*index=5*/f32[1...) fusion(f32[1536]{0:T(1024)S(1)} %get-tuple-element.515, ...), kind=kLoop, calls=%fused_computation.94.clone.1 | loop fusion | flops 202881024 | bytes 147456 | tf_op jit(solution)/shard_map/while/body/eval_jaxpr/while/body/eval_jaxpr/reduce_sum | solution.py:49
  339.5 33.9 %fusion.84 = (f32[1536]{0:T(1024)S(1)}, f32[1536]{0:T(1024)S(1)}, f32[1536]{0:T(1024)S(1)}, f32[1536]{0:T(1024)S(1)}, f32[1536]{0:T(1024)S(1)}, /*index=5*/f32[1...) fusion(f32[1536]{0:T(1024)S(1)} %get-tuple-element.515, ...), kind=kLoop, calls=%fused_computation.94.clone.1 | loop fusion | flops 202881024 | bytes 147456 | tf_op jit(solution)/shard_map/while/body/eval_jaxpr/while/body/eval_jaxpr/reduce_sum | solution.py:49
  389.5 5.9 conditional.31
  400.3 69.0 %while.54 = (s32[]{:T(128)}, f32[2,6,1536]{2,1,0:T(8,128)S(1)}, f32[2,6,1536]{2,1,0:T(8,128)S(1)}, f32[2,6,1536]{2,1,0:T(8,128)S(1)}, f32[2,6,1536]{2,1,0:T(8,12...) while((s32[]{:T(128)}, f32[2,6,1536]{2,1,0:T(8,128)S(1)}, ...), condition=%wide.region_36.36_spmd, body=%wide.region_23.35_spmd.sunk | while | flops 202899456 | bytes 786661 | solution.py:77
  400.6 33.9 %fusion.84 = (f32[1536]{0:T(1024)S(1)}, f32[1536]{0:T(1024)S(1)}, f32[1536]{0:T(1024)S(1)}, f32[1536]{0:T(1024)S(1)}, f32[1536]{0:T(1024)S(1)}, /*index=5*/f32[1...) fusion(f32[1536]{0:T(1024)S(1)} %get-tuple-element.515, ...), kind=kLoop, calls=%fused_computation.94.clone.1 | loop fusion | flops 202881024 | bytes 147456 | tf_op jit(solution)/shard_map/while/body/eval_jaxpr/while/body/eval_jaxpr/reduce_sum | solution.py:49
  435.1 33.9 %fusion.84 = (f32[1536]{0:T(1024)S(1)}, f32[1536]{0:T(1024)S(1)}, f32[1536]{0:T(1024)S(1)}, f32[1536]{0:T(1024)S(1)}, f32[1536]{0:T(1024)S(1)}, /*index=5*/f32[1...) fusion(f32[1536]{0:T(1024)S(1)} %get-tuple-element.515, ...), kind=kLoop, calls=%fused_computation.94.clone.1 | loop fusion | flops 202881024 | bytes 147456 | tf_op jit(solution)/shard_map/while/body/eval_jaxpr/while/body/eval_jaxpr/reduce_sum | solution.py:49
  473.0 5.1 conditional.38
  480.1 11.0 %conditional.28 = (f32[6,3072]{1,0:T(8,128)}) conditional(s32[]{:T(128)} %bitcast.100, f32[6,3072]{1,0:T(8,128)S(1)} %get-tuple-element.659, f32[6,3072]{1,0:T(8,128)S(1)} %get-tuple-element.659), branch_computations={%region_9.9_spmd, %region_10.10_spmd} | conditional | bytes 294960 | solution.py:89
  480.1 9.9 %collective-permute-start = (f32[6,3072]{1,0:T(8,128)S(1)}, f32[6,3072]{1,0:T(8,128)}, u32[]{:S(2)}, u32[]{:S(2)}) collective-permute-start(f32[6,3072]{1,0:T(8,128)S(1)} %param.3), channel_id=1, source_target_pairs={{0,1},{1,0},{2,3},{3,2},{4,5},{5,4},{6,7},{7,6},{8,9},{9,8},{10,11... | collective-permute-start | bytes 221192 | tf_op jit(solution)/shard_map/while/body/eval_jaxpr/cond/branch_1_fun/ppermute | solution.py:14
  491.1 4.9 conditional.29
  502.2 69.0 %while.54 = (s32[]{:T(128)}, f32[2,6,1536]{2,1,0:T(8,128)S(1)}, f32[2,6,1536]{2,1,0:T(8,128)S(1)}, f32[2,6,1536]{2,1,0:T(8,128)S(1)}, f32[2,6,1536]{2,1,0:T(8,12...) while((s32[]{:T(128)}, f32[2,6,1536]{2,1,0:T(8,128)S(1)}, ...), condition=%wide.region_36.36_spmd, body=%wide.region_23.35_spmd.sunk | while | flops 202899456 | bytes 786661 | solution.py:77
  502.5 33.9 %fusion.84 = (f32[1536]{0:T(1024)S(1)}, f32[1536]{0:T(1024)S(1)}, f32[1536]{0:T(1024)S(1)}, f32[1536]{0:T(1024)S(1)}, f32[1536]{0:T(1024)S(1)}, /*index=5*/f32[1...) fusion(f32[1536]{0:T(1024)S(1)} %get-tuple-element.515, ...), kind=kLoop, calls=%fused_computation.94.clone.1 | loop fusion | flops 202881024 | bytes 147456 | tf_op jit(solution)/shard_map/while/body/eval_jaxpr/while/body/eval_jaxpr/reduce_sum | solution.py:49
  537.0 33.9 %fusion.84 = (f32[1536]{0:T(1024)S(1)}, f32[1536]{0:T(1024)S(1)}, f32[1536]{0:T(1024)S(1)}, f32[1536]{0:T(1024)S(1)}, f32[1536]{0:T(1024)S(1)}, /*index=5*/f32[1...) fusion(f32[1536]{0:T(1024)S(1)} %get-tuple-element.515, ...), kind=kLoop, calls=%fused_computation.94.clone.1 | loop fusion | flops 202881024 | bytes 147456 | tf_op jit(solution)/shard_map/while/body/eval_jaxpr/while/body/eval_jaxpr/reduce_sum | solution.py:49
  587.3 6.6 conditional.33
  597.5 69.0 %while.54 = (s32[]{:T(128)}, f32[2,6,1536]{2,1,0:T(8,128)S(1)}, f32[2,6,1536]{2,1,0:T(8,128)S(1)}, f32[2,6,1536]{2,1,0:T(8,128)S(1)}, f32[2,6,1536]{2,1,0:T(8,12...) while((s32[]{:T(128)}, f32[2,6,1536]{2,1,0:T(8,128)S(1)}, ...), condition=%wide.region_36.36_spmd, body=%wide.region_23.35_spmd.sunk | while | flops 202899456 | bytes 786661 | solution.py:77
  597.8 33.9 %fusion.84 = (f32[1536]{0:T(1024)S(1)}, f32[1536]{0:T(1024)S(1)}, f32[1536]{0:T(1024)S(1)}, f32[1536]{0:T(1024)S(1)}, f32[1536]{0:T(1024)S(1)}, /*index=5*/f32[1...) fusion(f32[1536]{0:T(1024)S(1)} %get-tuple-element.515, ...), kind=kLoop, calls=%fused_computation.94.clone.1 | loop fusion | flops 202881024 | bytes 147456 | tf_op jit(solution)/shard_map/while/body/eval_jaxpr/while/body/eval_jaxpr/reduce_sum | solution.py:49
  632.3 33.9 %fusion.84 = (f32[1536]{0:T(1024)S(1)}, f32[1536]{0:T(1024)S(1)}, f32[1536]{0:T(1024)S(1)}, f32[1536]{0:T(1024)S(1)}, f32[1536]{0:T(1024)S(1)}, /*index=5*/f32[1...) fusion(f32[1536]{0:T(1024)S(1)} %get-tuple-element.515, ...), kind=kLoop, calls=%fused_computation.94.clone.1 | loop fusion | flops 202881024 | bytes 147456 | tf_op jit(solution)/shard_map/while/body/eval_jaxpr/while/body/eval_jaxpr/reduce_sum | solution.py:49
  670.2 5.1 conditional.40
  683.6 6.8 conditional.31
  695.4 69.0 %while.54 = (s32[]{:T(128)}, f32[2,6,1536]{2,1,0:T(8,128)S(1)}, f32[2,6,1536]{2,1,0:T(8,128)S(1)}, f32[2,6,1536]{2,1,0:T(8,128)S(1)}, f32[2,6,1536]{2,1,0:T(8,12...) while((s32[]{:T(128)}, f32[2,6,1536]{2,1,0:T(8,128)S(1)}, ...), condition=%wide.region_36.36_spmd, body=%wide.region_23.35_spmd.sunk | while | flops 202899456 | bytes 786661 | solution.py:77
  695.6 33.9 %fusion.84 = (f32[1536]{0:T(1024)S(1)}, f32[1536]{0:T(1024)S(1)}, f32[1536]{0:T(1024)S(1)}, f32[1536]{0:T(1024)S(1)}, f32[1536]{0:T(1024)S(1)}, /*index=5*/f32[1...) fusion(f32[1536]{0:T(1024)S(1)} %get-tuple-element.515, ...), kind=kLoop, calls=%fused_computation.94.clone.1 | loop fusion | flops 202881024 | bytes 147456 | tf_op jit(solution)/shard_map/while/body/eval_jaxpr/while/body/eval_jaxpr/reduce_sum | solution.py:49
  730.1 33.9 %fusion.84 = (f32[1536]{0:T(1024)S(1)}, f32[1536]{0:T(1024)S(1)}, f32[1536]{0:T(1024)S(1)}, f32[1536]{0:T(1024)S(1)}, f32[1536]{0:T(1024)S(1)}, /*index=5*/f32[1...) fusion(f32[1536]{0:T(1024)S(1)} %get-tuple-element.515, ...), kind=kLoop, calls=%fused_computation.94.clone.1 | loop fusion | flops 202881024 | bytes 147456 | tf_op jit(solution)/shard_map/while/body/eval_jaxpr/while/body/eval_jaxpr/reduce_sum | solution.py:49
  768.0 5.1 conditional.38
  768.6 4.5 collective-permute-done.10
  777.0 6.2 conditional.31
  777.7 5.0 collective-permute-done.3
  783.9 4.4 conditional.32
  792.6 69.0 %while.54 = (s32[]{:T(128)}, f32[2,6,1536]{2,1,0:T(8,128)S(1)}, f32[2,6,1536]{2,1,0:T(8,128)S(1)}, f32[2,6,1536]{2,1,0:T(8,128)S(1)}, f32[2,6,1536]{2,1,0:T(8,12...) while((s32[]{:T(128)}, f32[2,6,1536]{2,1,0:T(8,128)S(1)}, ...), condition=%wide.region_36.36_spmd, body=%wide.region_23.35_spmd.sunk | while | flops 202899456 | bytes 786661 | solution.py:77
  792.9 33.9 %fusion.84 = (f32[1536]{0:T(1024)S(1)}, f32[1536]{0:T(1024)S(1)}, f32[1536]{0:T(1024)S(1)}, f32[1536]{0:T(1024)S(1)}, f32[1536]{0:T(1024)S(1)}, /*index=5*/f32[1...) fusion(f32[1536]{0:T(1024)S(1)} %get-tuple-element.515, ...), kind=kLoop, calls=%fused_computation.94.clone.1 | loop fusion | flops 202881024 | bytes 147456 | tf_op jit(solution)/shard_map/while/body/eval_jaxpr/while/body/eval_jaxpr/reduce_sum | solution.py:49
  827.4 33.9 %fusion.84 = (f32[1536]{0:T(1024)S(1)}, f32[1536]{0:T(1024)S(1)}, f32[1536]{0:T(1024)S(1)}, f32[1536]{0:T(1024)S(1)}, f32[1536]{0:T(1024)S(1)}, /*index=5*/f32[1...) fusion(f32[1536]{0:T(1024)S(1)} %get-tuple-element.515, ...), kind=kLoop, calls=%fused_computation.94.clone.1 | loop fusion | flops 202881024 | bytes 147456 | tf_op jit(solution)/shard_map/while/body/eval_jaxpr/while/body/eval_jaxpr/reduce_sum | solution.py:49
  861.7 5.1 conditional.38
  871.1 75.8 %pmax.7 = f32[]{:T(128)} all-reduce(f32[]{:T(128)} %reduce_max.9), channel_id=1, replica_groups=mesh['grp'=2,'dev'=64] {'grp','dev'}, use_global_device_ids=true, to_apply=%region_54.55 | all-reduce | flops 1 | bytes 8 | tf_op jit(solution)/shard_map/pmax | solution.py:114
  (560 shorter events, 227.8 us)
Async XLA Ops:
  1.3 0.9 copy-start
  1.3 0.9 copy-start.1
  2.2 99.3 %copy-start.2 = (s32[8,1]{0,1:T(1,128)S(1)}, s32[8,1]{0,1:T(1,128)}, u32[]{:S(2)}) copy-start(s32[8,1]{0,1:T(1,128)} %param.39) | copy-start | bytes 100
  103.6 2.6 collective-permute-start
  109.4 5.9 collective-permute-start.6
  188.0 2.2 collective-permute-start.7
  190.3 5.6 collective-permute-start.13
  197.9 2.4 collective-permute-start
  200.9 4.3 collective-permute-start.2
  280.5 2.2 collective-permute-start.7
  282.8 4.1 collective-permute-start.9
  289.5 3.7 collective-permute-start.1
  295.8 4.0 collective-permute-start.4
  373.8 3.5 collective-permute-start.8
  377.4 3.8 collective-permute-start.11
  383.9 3.7 collective-permute-start.1
  389.5 5.3 collective-permute-start.3
  469.4 3.5 collective-permute-start.8
  473.0 5.1 collective-permute-start.10
  480.1 11.0 %collective-permute-start = (f32[6,3072]{1,0:T(8,128)S(1)}, f32[6,3072]{1,0:T(8,128)}, u32[]{:S(2)}, u32[]{:S(2)}) collective-permute-start(f32[6,3072]{1,0:T(8,128)S(1)} %param.3), channel_id=1, source_target_pairs={{0,1},{1,0},{2,3},{3,2},{4,5},{5,4},{6,7},{7,6},{8,9},{9,8},{10,11... | collective-permute-start | bytes 221192 | tf_op jit(solution)/shard_map/while/body/eval_jaxpr/cond/branch_1_fun/ppermute | solution.py:14
  491.1 4.2 collective-permute-start.1
  571.3 2.2 collective-permute-start.7
  573.5 4.1 collective-permute-start.8
  581.0 3.8 collective-permute-start.2
  587.3 6.0 collective-permute-start.5
  666.6 3.5 collective-permute-start.9
  670.3 5.1 collective-permute-start.12
  678.6 3.8 collective-permute-start.2
  683.6 6.2 collective-permute-start.3
  764.5 3.5 collective-permute-start.9
  768.0 5.1 collective-permute-start.10
  777.1 5.6 collective-permute-start.3
  783.9 3.8 collective-permute-start.4
  861.8 5.1 collective-permute-start.10
  866.8 3.5 collective-permute-start.11
where the time goes:
time: 950 us; the launch traced here: 948 us
  other arithmetic  652 us (69%)
  waiting for transfers between devices  87.8 us (9%)
  blocking collectives  75.8 us (8%)
  starting transfers between devices  50.4 us (5%)
  loops' own time  45.6 us (5%)
  local copies, waits for them, and re-layouts  35.2 us (4%)
    reduce_sum x16, other arithmetic, pair_terms(): jnp.sum(fifth * source_along * back_swirl[component] - cube * spin[compon...  542 us
    reduce_sum x3, other arithmetic, pair_terms(): jnp.sum(cube * spin[component] - fifth * along * swirl[component], 1)  98.7 us
    ppermute x32, waiting for transfers between devices, partner(): lax.ppermute(shard, axis, [(i, i ^ 1 << stride) for i in range(lax.axis_s...  87.8 us
    pmax x1, blocking collectives, body(): peak_sq = lax.pmax(local_peak, ('grp', 'dev'))  75.8 us
    ppermute x32, starting transfers between devices, partner(): lax.ppermute(shard, axis, [(i, i ^ 1 << stride) for i in range(lax.axis_s...  50.4 us
    another operation x1, loops' own time, body(): totals = lax.fori_loop(0, rounds, home_round, totals)  42.1 us
  transfers between devices with their start and end apart: 32, of which 32 were waited for; matrix products, arithmetic and copies ran while one was open for 0% of the time, Pallas kernels for 0%

commit v1 on v0

v1 whole, which is shorter than its diff:
```python
import functools
import math

import jax
import jax.numpy as jnp
from jax import lax
from jax.experimental import pallas as pl
from jax.experimental.pallas import tpu as pltpu
from jax.sharding import PartitionSpec as P

SMOOTH_SQ = 0.01
INV_FOUR_PI = 1.0 / (4.0 * math.pi)
STEP_RATE = 0.25
AXES = ("grp", "dev")
TILE = 1024
CHUNK = 512
PIECE = 64
LANES = 256
K_DIST = 48
ROWS3 = 32
ROWS5 = 80
BF16 = jnp.bfloat16
F32 = jnp.float32


def dot(left, right):
    return jnp.dot(left, right, preferred_element_type=F32)


def pieces(value, dtype, count):
    out = []
    for _ in range(count):
        head = value.astype(dtype).astype(F32)
        out.append(head)
        value = value - head
    return out


def cross_rows(first, second):
    return [
        first[1] * second[2] - first[2] * second[1],
        first[2] * second[0] - first[0] * second[2],
        first[0] * second[1] - first[1] * second[0],
    ]


def rows_of(block):
    return [block[k : k + 1, :] for k in range(block.shape[0])]


def pair_kernel(
    slots, pick_ref, src_ref, home_ref, carry_ref, out_ref, peak_ref,
    feat3, feat5, dist8, fs, ft, x3, x5, o3, o5, *bufs
):
    count = home_ref.shape[1]
    chunks = slots * count // CHUNK
    tiles = count // TILE
    first, second = bufs[:4], bufs[4:]

    largest = jnp.max(jnp.abs(src_ref[pick_ref[0], 3:6, :]))
    for slot in range(1, slots):
        largest = jnp.maximum(largest, jnp.max(jnp.abs(src_ref[pick_ref[slot], 3:6, :])))
    scale = jnp.maximum(largest, 1e-30)

    feat3[...] = jnp.zeros_like(feat3)
    dist8[...] = jnp.zeros_like(dist8)

    def fill(slot, _):
        block = src_ref[pick_ref[slot]]
        cols = pl.ds(pl.multiple_of(slot * count, count), count)
        pos = rows_of(block[0:3])
        strength = rows_of(block[3:6] / scale)
        moment = cross_rows(pos, strength)
        for k in range(3):
            feat3[k : k + 1, :] = strength[k]
            feat3[3 + k : 4 + k, :] = moment[k]
            feat5[k : k + 1, :] = strength[k]
            feat5[3 + k : 4 + k, :] = moment[k]
            for l in range(3):
                feat5[6 + 3 * k + l : 7 + 3 * k + l, :] = pos[k] * strength[l]
                feat5[15 + 3 * k + l : 16 + 3 * k + l, :] = pos[k] * moment[l]
            dist8[k : k + 1, :] = pos[k]
        dist8[3:4, :] = pos[0] * pos[0] + pos[1] * pos[1] + pos[2] * pos[2]
        dist8[4:5, :] = jnp.ones_like(pos[0])
        q = pieces(dist8[...], BF16, 3)
        rows = jnp.concatenate([q[0], q[0], q[1], q[1], q[0], q[2]], 0)
        rows = jnp.concatenate([rows, jnp.zeros((128 - K_DIST, count), F32)], 0)
        fs[cols, :] = rows.T.astype(BF16)
        f3 = feat3[...]
        f5 = feat5[...]
        p = pieces(f3, BF16, 3)
        x3[:, cols] = jnp.concatenate(p + [jnp.zeros_like(f3)], 0).astype(BF16)
        p = pieces(f5, BF16, 3)
        x5[:, cols] = jnp.concatenate(p + [jnp.zeros_like(f3)], 0).astype(BF16)
        return 0

    lax.fori_loop(0, slots, fill, 0)

    pos = [home_ref[k : k + 1, :] for k in range(3)]
    for k in range(3):
        dist8[k : k + 1, :] = -2.0 * pos[k]
    dist8[3:4, :] = jnp.ones_like(pos[0])
    dist8[4:5, :] = (pos[0] * pos[0] + pos[1] * pos[1] + pos[2] * pos[2]) + SMOOTH_SQ
    q = pieces(dist8[...], BF16, 3)
    rows = jnp.concatenate([q[0], q[1], q[0], q[1], q[2], q[0]], 0)
    ft[...] = rows.astype(BF16)
    o3[...] = jnp.zeros_like(o3)
    o5[...] = jnp.zeros_like(o5)

    def weigh(new, tile, chunk, part, rows_at):
        cols = pl.ds(pl.multiple_of(tile * TILE + part * LANES, LANES), LANES)
        rows = pl.ds(pl.multiple_of(chunk * CHUNK + rows_at, PIECE), PIECE)
        inverse = lax.rsqrt(dot(fs[rows, 0:K_DIST], ft[:, cols]))
        square = inverse * inverse
        cube = square * inverse
        fifth = cube * square
        at = (slice(rows_at, rows_at + PIECE), slice(part * LANES, (part + 1) * LANES))
        head = cube.astype(BF16)
        new[0][at] = head
        new[1][at] = (cube - head.astype(F32)).astype(BF16)
        head = fifth.astype(BF16)
        new[2][at] = head
        new[3][at] = (fifth - head.astype(F32)).astype(BF16)

    def gather(old, tile, chunk, part, which):
        cols = pl.ds(pl.multiple_of(tile * TILE + part * LANES, LANES), LANES)
        rows = pl.ds(pl.multiple_of(chunk * CHUNK, CHUNK), CHUNK)
        at = slice(part * LANES, (part + 1) * LANES)
        if which == 0:
            o3[:, cols] += dot(x3[:, rows], old[0][:, at])
        elif which == 1:
            o5[:, cols] += dot(x5[:, rows], old[2][:, at])
        elif which == 2:
            o3[0:16, cols] += dot(x3[0:16, rows], old[1][:, at])
        else:
            o5[0:48, cols] += dot(x5[0:48, rows], old[3][:, at])

    def step(index, new, old):
        following = jnp.minimum(index + 1, tiles * chunks - 1)
        new_tile, new_chunk = following // chunks, following % chunks
        tile, chunk = index // chunks, index % chunks
        each = CHUNK // PIECE // 4
        for part in range(TILE // LANES):
            for which in range(4):
                for number in range(each):
                    weigh(new, new_tile, new_chunk, part, (which * each + number) * PIECE)
                gather(old, tile, chunk, part, which)

    for part in range(TILE // LANES):
        for number in range(CHUNK // PIECE):
            weigh(first, 0, 0, part, number * PIECE)

    def two_steps(pair, _):
        step(2 * pair, second, first)
        step(2 * pair + 1, first, second)
        return 0

    lax.fori_loop(0, tiles * chunks // 2, two_steps, 0)

    sum3 = o3[0:8, :] + o3[8:16, :] + o3[16:24, :]
    sum5 = o5[0:24, :] + o5[24:48, :] + o5[48:72, :]
    factor = -INV_FOUR_PI * scale
    own = [home_ref[3 + k : 4 + k, :] for k in range(3)]
    spin = rows_of(sum3[0:3])
    turn = cross_rows(pos, spin)
    plain5 = rows_of(sum5[0:3])
    moment5 = rows_of(sum5[3:6])
    along = own[0] * pos[0] + own[1] * pos[1] + own[2] * pos[2]
    swirl, lever = [], []
    for l in range(3):
        total = along * plain5[l]
        other = along * moment5[l]
        for k in range(3):
            total -= own[k] * sum5[6 + 3 * k + l : 7 + 3 * k + l, :]
            other -= own[k] * sum5[15 + 3 * k + l : 16 + 3 * k + l, :]
        swirl.append(total)
        lever.append(other)
    twist = cross_rows(pos, swirl)
    tilt = cross_rows(own, spin)
    size = 0.0
    for k in range(3):
        row = factor * (turn[k] - sum3[3 + k : 4 + k, :])
        out_ref[k : k + 1, :] = row + carry_ref[k : k + 1, :]
        row = factor * (tilt[k] - 3.0 * (twist[k] - lever[k])) + carry_ref[3 + k : 4 + k, :]
        out_ref[3 + k : 4 + k, :] = row
        size += row * row
    peak_ref[...] = jnp.full(peak_ref.shape, jnp.max(size), F32)


def pair_sums(picks, sources, home, carry):
    slots, count = picks.shape[0], home.shape[1]
    total = slots * count
    buffers = [pltpu.VMEM((CHUNK, TILE), BF16)] * 8
    vmem = pl.BlockSpec(memory_space=pltpu.VMEM)
    return pl.pallas_call(
        functools.partial(pair_kernel, slots),
        out_shape=(
            jax.ShapeDtypeStruct((6, count), F32),
            jax.ShapeDtypeStruct((8, 128), F32),
        ),
        in_specs=[pl.BlockSpec(memory_space=pltpu.SMEM), vmem, vmem, vmem],
        out_specs=(vmem, vmem),
        scratch_shapes=[
            pltpu.VMEM((8, count), F32),
            pltpu.VMEM((24, count), F32),
            pltpu.VMEM((8, count), F32),
            pltpu.VMEM((total, 128), BF16),
            pltpu.VMEM((K_DIST, count), BF16),
            pltpu.VMEM((ROWS3, total), BF16),
            pltpu.VMEM((ROWS5, total), BF16),
            pltpu.VMEM((ROWS3, count), F32),
            pltpu.VMEM((ROWS5, count), F32),
        ]
        + buffers,
        compiler_params=pltpu.CompilerParams(vmem_limit_bytes=56 << 20),
    )(picks, sources, home, carry)


def flip(array, mask, devices):
    return lax.ppermute(array, AXES, [(i, i ^ mask) for i in range(devices)])


def visitors(home, devices):
    levels = devices.bit_length() - 1
    near = [flip(home, 1 << bit, devices) for bit in range(levels)]
    order = [bit for bit in (0, 1, 2, 4, 3, 5, 6) if bit < levels]
    order += [bit for bit in range(levels) if bit not in order]
    got, masks = [], []
    for place, last in enumerate(order[:-1]):
        others = order[place + 1 :]
        got.append(flip(jnp.stack([near[bit] for bit in others]), 1 << last, devices))
        masks += [1 << last | 1 << bit for bit in others]
    return jnp.concatenate(got, 0), masks


def body(positions, strengths, plan):
    devices = lax.axis_size(AXES)
    home = jnp.concatenate([positions, strengths], 0)
    blocks, masks = visitors(home, devices)
    own_masks = jnp.bitwise_xor(plan[:, 0], lax.axis_index(AXES).astype(jnp.int32))
    hits = own_masks[:, None] == jnp.asarray(masks, jnp.int32)[None, :]
    picks = jnp.sum(jnp.where(hits, jnp.arange(len(masks), dtype=jnp.int32)[None, :], 0), 1)
    nothing = jnp.zeros_like(home)
    partial, _ = pair_sums(jnp.zeros((1,), jnp.int32), home[None], home, nothing)
    totals, peaks = pair_sums(picks.astype(jnp.int32), blocks, home, partial)
    peak_sq = lax.pmax(peaks[0, 0], AXES)
    stretch = totals[3:]
    new_strengths = strengths + STEP_RATE / (jnp.sqrt(peak_sq) + 1e-06) * stretch
    return (totals[:3], new_strengths)


def solution(mesh):
    placed = (P(None, AXES), P(None, AXES), P(None, AXES))
    return jax.shard_map(
        body,
        mesh=mesh,
        in_specs=placed,
        out_specs=(P(None, AXES), P(None, AXES)),
        check_vma=False,
    )
```

time: 950 us -> 328 us (0.35)
  other arithmetic: 652 us -> 5.23 us
  Pallas kernels: 0 us -> 218 us
  waiting for transfers between devices: 87.8 us -> 16.1 us
  loops' own time: 45.6 us -> 0 us
  starting transfers between devices: 50.4 us -> 17.5 us
  local copies, waits for them, and re-layouts: 35.2 us -> 3.4 us
  blocking collectives: 75.8 us -> 65.9 us
    reduce_sum x20 -> x1, other arithmetic: 641 us -> 1.35 us  [body(): jnp.sum(jnp.where(hits, jnp.arange(len(masks), dtype=jnp.int32)[None, :],...]
    pallas_call x0 -> x2, Pallas kernels: none -> 218 us  [pair_sums(): pl.pallas_call(functools.partial(pair_kernel, slots), out_shape=(jax.Shap...]
    ppermute x32 -> x12, waiting for transfers between devices: 87.8 us -> 16.1 us  [flip(): return lax.ppermute(array, AXES, [(i, i ^ mask) for i in range(devices)])]
    another operation x122 -> x0, loops' own time: 45.6 us -> none  [the longest x1 42.1 us: body(): totals = lax.fori_loop(0, rounds, home_round, totals)]
    ppermute x32 -> x12, starting transfers between devices: 50.4 us -> 17.5 us  [flip(): return lax.ppermute(array, AXES, [(i, i ^ mask) for i in range(devices)])]
    cond x34 -> x0, local copies, waits for them, and re-layouts: 11.3 us -> none
    pmax x1, blocking collectives: 75.8 us -> 65.9 us  [body(): peak_sq = lax.pmax(peaks[0, 0], AXES)]
    dynamic_slice x16 -> x0, local copies, waits for them, and re-layouts: 9.73 us -> none  [the longest x8 4.89 us: home_round(): offset_mask = round_masks[round_no]]
  transfers between devices with their start and end apart: 32 -> 12, of which waited for: 32 -> 4; matrix products, arithmetic and copies ran while one was open for 0% -> 1% of each run, Pallas kernels for 0% -> 8%
where the time goes in v1:
time: 328 us
  Pallas kernels  218 us (66%)
  blocking collectives  65.9 us (20%)
  starting transfers between devices  17.5 us (5%)
  waiting for transfers between devices  16.1 us (5%)
  other arithmetic  5.23 us (2%)
  local copies, waits for them, and re-layouts  3.4 us (1%)
    pallas_call x2, Pallas kernels, pair_sums(): pl.pallas_call(functools.partial(pair_kernel, slots), out_shape=(jax.Shap...  218 us
    pmax x1, blocking collectives, body(): peak_sq = lax.pmax(peaks[0, 0], AXES)  65.9 us
    ppermute x12, starting transfers between devices, flip(): return lax.ppermute(array, AXES, [(i, i ^ mask) for i in range(devices)])  17.5 us
    ppermute x12, waiting for transfers between devices, flip(): return lax.ppermute(array, AXES, [(i, i ^ mask) for i in range(devices)])  16.1 us
  transfers between devices with their start and end apart: 12, of which 4 were waited for; matrix products, arithmetic and copies ran while one was open for 1% of the time, Pallas kernels for 8%

profile of v1, /device:TPU:1, one launch (start us, length us, event | category | flops | bytes accessed | tf_op | source)
XLA Modules:
  0.0 327.9 jit_solution(1375147698636548091)
XLA Ops:
  0.6 1.5 fusion
  2.1 0.0 copy-start.1
  2.1 2.1 collective-permute-start
  4.3 1.2 collective-permute-start.1
  5.5 1.6 collective-permute-start.2
  7.1 2.5 collective-permute-start.3
  9.6 3.3 %collective-permute-start.4 = (f32[6,3072]{1,0:T(8,128)S(1)}, f32[6,3072]{1,0:T(8,128)S(1)}, u32[]{:S(2)}, u32[]{:S(2)}) collective-permute-start(f32[6,3072]{1,0:T(8,128)S(1)} %get-tuple-element.11.home_ref), channel_id=1, source_target_pairs={{0,32},{1,33},{2,34},{3,35},{4,36},{5,37},{6,38},{7,39},{8,40},{9,... | collective-permute-start | bytes 221192 | tf_op jit(solution)/shard_map/ppermute | solution.py:220
  12.9 0.7 xor_bitcast_fusion
  13.5 0.6 broadcast_in_dim.24.carry_ref
  14.2 0.0 copy-done.1
  14.2 26.4 %shard_map.59 = (f32[6,3072]{1,0:T(8,128)}, f32[8,128]{1,0:T(8,128)}) custom-call(s32[1]{0:T(128)} %constant.9.clone.1.pick_ref, f32[1,6,3072]{2,1,0:T(8,128)} %get-tuple-element.10.src_ref, f32[6,3072]{1,0:T(8,128)} %copy-done.1, f32[6,3072]{1,0:T(8,128)} %broadcast_in_dim.24.carry_ref), custom_call_target="tpu_custom_call" | custom-call | tf_op jit(solution)/shard_map/pallas_call | solution.py:195
  40.5 1.3 select_reduce_fusion.pick_ref
  41.9 0.0 collective-permute-done
  41.9 2.6 collective-permute-start.5
  44.5 0.0 collective-permute-done.1
  44.5 0.0 collective-permute-done.2
  44.6 0.0 collective-permute-done.3
  44.6 0.0 collective-permute-done.4
  44.6 2.4 collective-permute-done.5
  47.1 3.3 %collective-permute-start.6 = (f32[6,6,3072]{2,1,0:T(8,128)S(1)}, f32[6,6,3072]{2,1,0:T(8,128)S(1)}, u32[]{:S(2)}, u32[]{:S(2)}) collective-permute-start(f32[6,6,3072]{2,1,0:T(8,128)S(1)} %get-tuple-element.13), channel_id=1, source_target_pairs={{0,1},{1,0},{2,3},{3,2},{4,5},{5,4},{6,7},{7,6},{8,9},{9,8},{10,11... | collective-permute-start | bytes 1327112 | tf_op jit(solution)/shard_map/ppermute | solution.py:220
  50.4 0.2 collective-permute-start.7
  50.6 0.0 collective-permute-start.11
  50.7 0.1 collective-permute-start.8
  50.8 0.1 collective-permute-start.9
  50.9 1.1 collective-permute-done.6
  52.0 0.5 collective-permute-start.10
  52.6 10.6 %collective-permute-done.7 = f32[5,6,3072]{2,1,0:T(8,128)S(1)} collective-permute-done((f32[5,6,3072]{2,1,0:T(8,128)S(1)}, f32[5,6,3072]{2,1,0:T(8,128)S(1)}, u32[]{:S(2)}, u32[]{:S(2)}) %collective-permute-start.7) | collective-permute-done | bytes 368672 | tf_op jit(solution)/shard_map/ppermute | solution.py:220
  63.2 0.0 copy-start.2
  63.2 0.0 collective-permute-done.8
  63.2 0.0 collective-permute-done.9
  63.3 1.9 collective-permute-done.10
  65.2 0.0 collective-permute-done.11
  65.3 0.0 copy-start
  65.3 1.3 copy-done
  66.6 191.8 %shard_map.60 = (f32[6,3072]{1,0:T(8,128)}, f32[8,128]{1,0:T(8,128)}) custom-call(s32[8]{0:T(128)} %select_reduce_fusion.pick_ref, f32[21,6,3072]{2,1,0:T(8,128)} %copy-done, f32[6,3072]{1,0:T(8,128)} %copy-done.1, f32[6,3072]{1,0:T(8,128)} %get-tuple-element.5.carry_ref), custom_call_target="tpu_custom_call" | custom-call | tf_op jit(solution)/shard_map/pallas_call | solution.py:195
  258.4 1.2 slice.10
  259.6 65.9 %pmax.7 = f32[]{:T(128)} all-reduce(f32[]{:T(128)} %bitcast.8), channel_id=1, replica_groups=mesh['grp'=2,'dev'=64] {'grp','dev'}, use_global_device_ids=true, to_apply=%region_1.2 | all-reduce | flops 1 | bytes 8 | tf_op jit(solution)/shard_map/pmax | solution.py:246
  326.2 0.0 copy-done.2
  326.2 1.6 multiply_add_fusion
  (15 shorter events, 0.3 us)
Async XLA Ops:
  2.1 12.0 %copy-start.1 = (f32[6,3072]{1,0:T(8,128)}, f32[6,3072]{1,0:T(8,128)S(1)}, u32[]{:S(2)}) copy-start(f32[6,3072]{1,0:T(8,128)S(1)} %get-tuple-element.11.home_ref) | copy-start | bytes 221188
  2.1 39.7 %collective-permute-start = (f32[6,3072]{1,0:T(8,128)S(1)}, f32[6,3072]{1,0:T(8,128)S(1)}, u32[]{:S(2)}, u32[]{:S(2)}) collective-permute-start(f32[6,3072]{1,0:T(8,128)S(1)} %get-tuple-element.11.home_ref), channel_id=1, source_target_pairs={{0,2},{1,3},{2,0},{3,1},{4,6},{5,7},{6,4},{7,5},{8,10},{9,11},{10,... | collective-permute-start | bytes 221192 | tf_op jit(solution)/shard_map/ppermute | solution.py:220
  4.3 40.3 %collective-permute-start.1 = (f32[6,3072]{1,0:T(8,128)S(1)}, f32[6,3072]{1,0:T(8,128)S(1)}, u32[]{:S(2)}, u32[]{:S(2)}) collective-permute-start(f32[6,3072]{1,0:T(8,128)S(1)} %get-tuple-element.11.home_ref), channel_id=1, source_target_pairs={{0,4},{1,5},{2,6},{3,7},{4,0},{5,1},{6,2},{7,3},{8,12},{9,13},{10,... | collective-permute-start | bytes 221192 | tf_op jit(solution)/shard_map/ppermute | solution.py:220
  5.5 39.1 %collective-permute-start.2 = (f32[6,3072]{1,0:T(8,128)S(1)}, f32[6,3072]{1,0:T(8,128)S(1)}, u32[]{:S(2)}, u32[]{:S(2)}) collective-permute-start(f32[6,3072]{1,0:T(8,128)S(1)} %get-tuple-element.11.home_ref), channel_id=1, source_target_pairs={{0,16},{1,17},{2,18},{3,19},{4,20},{5,21},{6,22},{7,23},{8,24},{9,... | collective-permute-start | bytes 221192 | tf_op jit(solution)/shard_map/ppermute | solution.py:220
  7.1 37.5 %collective-permute-start.3 = (f32[6,3072]{1,0:T(8,128)S(1)}, f32[6,3072]{1,0:T(8,128)S(1)}, u32[]{:S(2)}, u32[]{:S(2)}) collective-permute-start(f32[6,3072]{1,0:T(8,128)S(1)} %get-tuple-element.11.home_ref), channel_id=1, source_target_pairs={{0,8},{1,9},{2,10},{3,11},{4,12},{5,13},{6,14},{7,15},{8,0},{9,1},... | collective-permute-start | bytes 221192 | tf_op jit(solution)/shard_map/ppermute | solution.py:220
  9.6 35.0 %collective-permute-start.4 = (f32[6,3072]{1,0:T(8,128)S(1)}, f32[6,3072]{1,0:T(8,128)S(1)}, u32[]{:S(2)}, u32[]{:S(2)}) collective-permute-start(f32[6,3072]{1,0:T(8,128)S(1)} %get-tuple-element.11.home_ref), channel_id=1, source_target_pairs={{0,32},{1,33},{2,34},{3,35},{4,36},{5,37},{6,38},{7,39},{8,40},{9,... | collective-permute-start | bytes 221192 | tf_op jit(solution)/shard_map/ppermute | solution.py:220
  41.9 5.2 %collective-permute-start.5 = (f32[6,3072]{1,0:T(8,128)}, f32[6,3072]{1,0:T(8,128)S(1)}, u32[]{:S(2)}, u32[]{:S(2)}) collective-permute-start(f32[6,3072]{1,0:T(8,128)} %copy-done.1), channel_id=1, source_target_pairs={{0,64},{1,65},{2,66},{3,67},{4,68},{5,69},{6,70},{7,71},{8,72},{9,... | collective-permute-start | bytes 221192 | tf_op jit(solution)/shard_map/ppermute | solution.py:220
  47.1 4.9 %collective-permute-start.6 = (f32[6,6,3072]{2,1,0:T(8,128)S(1)}, f32[6,6,3072]{2,1,0:T(8,128)S(1)}, u32[]{:S(2)}, u32[]{:S(2)}) collective-permute-start(f32[6,6,3072]{2,1,0:T(8,128)S(1)} %get-tuple-element.13), channel_id=1, source_target_pairs={{0,1},{1,0},{2,3},{3,2},{4,5},{5,4},{6,7},{7,6},{8,9},{9,8},{10,11... | collective-permute-start | bytes 1327112 | tf_op jit(solution)/shard_map/ppermute | solution.py:220
  50.4 12.8 %collective-permute-start.7 = (f32[5,6,3072]{2,1,0:T(8,128)S(1)}, f32[5,6,3072]{2,1,0:T(8,128)S(1)}, u32[]{:S(2)}, u32[]{:S(2)}) collective-permute-start(f32[5,6,3072]{2,1,0:T(8,128)S(1)} %get-tuple-element.12), channel_id=1, source_target_pairs={{0,2},{1,3},{2,0},{3,1},{4,6},{5,7},{6,4},{7,5},{8,10},{9,11},{10,... | collective-permute-start | bytes 1105928 | tf_op jit(solution)/shard_map/ppermute | solution.py:220
  50.6 14.7 %collective-permute-start.11 = (f32[1,6,3072]{2,1,0:T(8,128)S(1)}, f32[1,6,3072]{2,1,0:T(8,128)S(1)}, u32[]{:S(2)}, u32[]{:S(2)}) collective-permute-start(f32[1,6,3072]{2,1,0:T(8,128)S(1)} %bitcast.22), channel_id=1, source_target_pairs={{0,32},{1,33},{2,34},{3,35},{4,36},{5,37},{6,38},{7,39},{8,40},{9,... | collective-permute-start | bytes 221192 | tf_op jit(solution)/shard_map/ppermute | solution.py:220
  50.7 12.5 %collective-permute-start.8 = (f32[4,6,3072]{2,1,0:T(8,128)S(1)}, f32[4,6,3072]{2,1,0:T(8,128)S(1)}, u32[]{:S(2)}, u32[]{:S(2)}) collective-permute-start(f32[4,6,3072]{2,1,0:T(8,128)S(1)} %pad_maximum_fusion), channel_id=1, source_target_pairs={{0,4},{1,5},{2,6},{3,7},{4,0},{5,1},{6,2},{7,3},{8,12},{9,13},{10,... | collective-permute-start | bytes 884744 | tf_op jit(solution)/shard_map/ppermute | solution.py:220
  50.8 12.5 %collective-permute-start.9 = (f32[3,6,3072]{2,1,0:T(8,128)S(1)}, f32[3,6,3072]{2,1,0:T(8,128)S(1)}, u32[]{:S(2)}, u32[]{:S(2)}) collective-permute-start(f32[3,6,3072]{2,1,0:T(8,128)S(1)} %pad_maximum_fusion.1), channel_id=1, source_target_pairs={{0,16},{1,17},{2,18},{3,19},{4,20},{5,21},{6,22},{7,23},{8,24},{9,... | collective-permute-start | bytes 663560 | tf_op jit(solution)/shard_map/ppermute | solution.py:220
  52.0 13.2 %collective-permute-start.10 = (f32[2,6,3072]{2,1,0:T(8,128)S(1)}, f32[2,6,3072]{2,1,0:T(8,128)S(1)}, u32[]{:S(2)}, u32[]{:S(2)}) collective-permute-start(f32[2,6,3072]{2,1,0:T(8,128)S(1)} %pad_maximum_fusion.2), channel_id=1, source_target_pairs={{0,8},{1,9},{2,10},{3,11},{4,12},{5,13},{6,14},{7,15},{8,0},{9,1},... | collective-permute-start | bytes 442376 | tf_op jit(solution)/shard_map/ppermute | solution.py:220
  63.2 263.0 %copy-start.2 = (f32[3,3072]{1,0:T(4,128)S(1)}, f32[3,3072]{1,0:T(4,128)}, u32[]{:S(2)}) copy-start(f32[3,3072]{1,0:T(4,128)} %param.5) | copy-start | bytes 110596
  65.3 1.3 copy-start

commit v2 on v1

--- a/solution.py
+++ b/solution.py
@@ -12,12 +12,11 @@
 INV_FOUR_PI = 1.0 / (4.0 * math.pi)
 STEP_RATE = 0.25
 AXES = ("grp", "dev")
-TILE = 1024
-CHUNK = 512
+TILE = 256
 PIECE = 64
 LANES = 256
 K_DIST = 48
-ROWS3 = 32
+ROWS3 = 16
 ROWS5 = 80
 BF16 = jnp.bfloat16
 F32 = jnp.float32
@@ -49,11 +48,12 @@
 
 
 def pair_kernel(
-    slots, pick_ref, src_ref, home_ref, carry_ref, out_ref, peak_ref,
+    slots, chunk_size, pick_ref, src_ref, home_ref, carry_ref, out_ref, peak_ref,
     feat3, feat5, dist8, fs, ft, x3, x5, o3, o5, *bufs
 ):
     count = home_ref.shape[1]
-    chunks = slots * count // CHUNK
+    width = src_ref.shape[2]
+    chunks = slots * width // chunk_size
     tiles = count // TILE
     first, second = bufs[:4], bufs[4:]
 
@@ -67,7 +67,7 @@
 
     def fill(slot, _):
         block = src_ref[pick_ref[slot]]
-        cols = pl.ds(pl.multiple_of(slot * count, count), count)
+        cols = pl.ds(pl.multiple_of(slot * width, width), width)
         pos = rows_of(block[0:3])
         strength = rows_of(block[3:6] / scale)
         moment = cross_rows(pos, strength)
@@ -79,17 +79,16 @@
             for l in range(3):
                 feat5[6 + 3 * k + l : 7 + 3 * k + l, :] = pos[k] * strength[l]
                 feat5[15 + 3 * k + l : 16 + 3 * k + l, :] = pos[k] * moment[l]
-            dist8[k : k + 1, :] = pos[k]
-        dist8[3:4, :] = pos[0] * pos[0] + pos[1] * pos[1] + pos[2] * pos[2]
-        dist8[4:5, :] = jnp.ones_like(pos[0])
-        q = pieces(dist8[...], BF16, 3)
+            dist8[k : k + 1, 0:width] = pos[k]
+        dist8[3:4, 0:width] = pos[0] * pos[0] + pos[1] * pos[1] + pos[2] * pos[2]
+        dist8[4:5, 0:width] = jnp.ones_like(pos[0])
+        q = pieces(dist8[:, 0:width], BF16, 3)
         rows = jnp.concatenate([q[0], q[0], q[1], q[1], q[0], q[2]], 0)
-        rows = jnp.concatenate([rows, jnp.zeros((128 - K_DIST, count), F32)], 0)
+        rows = jnp.concatenate([rows, jnp.zeros((128 - K_DIST, width), F32)], 0)
         fs[cols, :] = rows.T.astype(BF16)
         f3 = feat3[...]
         f5 = feat5[...]
-        p = pieces(f3, BF16, 3)
-        x3[:, cols] = jnp.concatenate(p + [jnp.zeros_like(f3)], 0).astype(BF16)
+        x3[:, cols] = jnp.concatenate(pieces(f3, BF16, 2), 0).astype(BF16)
         p = pieces(f5, BF16, 3)
         x5[:, cols] = jnp.concatenate(p + [jnp.zeros_like(f3)], 0).astype(BF16)
         return 0
@@ -109,7 +108,7 @@
 
     def weigh(new, tile, chunk, part, rows_at):
         cols = pl.ds(pl.multiple_of(tile * TILE + part * LANES, LANES), LANES)
-        rows = pl.ds(pl.multiple_of(chunk * CHUNK + rows_at, PIECE), PIECE)
+        rows = pl.ds(pl.multiple_of(chunk * chunk_size + rows_at, PIECE), PIECE)
         inverse = lax.rsqrt(dot(fs[rows, 0:K_DIST], ft[:, cols]))
         square = inverse * inverse
         cube = square * inverse
@@ -124,7 +123,7 @@
 
     def gather(old, tile, chunk, part, which):
         cols = pl.ds(pl.multiple_of(tile * TILE + part * LANES, LANES), LANES)
-        rows = pl.ds(pl.multiple_of(chunk * CHUNK, CHUNK), CHUNK)
+        rows = pl.ds(pl.multiple_of(chunk * chunk_size, chunk_size), chunk_size)
         at = slice(part * LANES, (part + 1) * LANES)
         if which == 0:
             o3[:, cols] += dot(x3[:, rows], old[0][:, at])
@@ -139,7 +138,7 @@
         following = jnp.minimum(index + 1, tiles * chunks - 1)
         new_tile, new_chunk = following // chunks, following % chunks
         tile, chunk = index // chunks, index % chunks
-        each = CHUNK // PIECE // 4
+        each = chunk_size // PIECE // 4
         for part in range(TILE // LANES):
             for which in range(4):
                 for number in range(each):
@@ -147,7 +146,7 @@
                 gather(old, tile, chunk, part, which)
 
     for part in range(TILE // LANES):
-        for number in range(CHUNK // PIECE):
+        for number in range(chunk_size // PIECE):
             weigh(first, 0, 0, part, number * PIECE)
 
     def two_steps(pair, _):
@@ -157,7 +156,7 @@
 
     lax.fori_loop(0, tiles * chunks // 2, two_steps, 0)
 
-    sum3 = o3[0:8, :] + o3[8:16, :] + o3[16:24, :]
+    sum3 = o3[0:8, :] + o3[8:16, :]
     sum5 = o5[0:24, :] + o5[24:48, :] + o5[48:72, :]
     factor = -INV_FOUR_PI * scale
     own = [home_ref[3 + k : 4 + k, :] for k in range(3)]
@@ -187,22 +186,22 @@
     peak_ref[...] = jnp.full(peak_ref.shape, jnp.max(size), F32)
 
 
-def pair_sums(picks, sources, home, carry):
-    slots, count = picks.shape[0], home.shape[1]
-    total = slots * count
-    buffers = [pltpu.VMEM((CHUNK, TILE), BF16)] * 8
+def pair_sums(picks, sources, home, carry, chunk_size=1024):
+    slots, width, count = picks.shape[0], sources.shape[2], home.shape[1]
+    total = slots * width
+    buffers = [pltpu.VMEM((chunk_size, TILE), BF16)] * 8
     vmem = pl.BlockSpec(memory_space=pltpu.VMEM)
     return pl.pallas_call(
-        functools.partial(pair_kernel, slots),
+        functools.partial(pair_kernel, slots, chunk_size),
         out_shape=(
             jax.ShapeDtypeStruct((6, count), F32),
-            jax.ShapeDtypeStruct((8, 128), F32),
+            jax.ShapeDtypeStruct((128, 128), F32),
         ),
         in_specs=[pl.BlockSpec(memory_space=pltpu.SMEM), vmem, vmem, vmem],
         out_specs=(vmem, vmem),
         scratch_shapes=[
-            pltpu.VMEM((8, count), F32),
-            pltpu.VMEM((24, count), F32),
+            pltpu.VMEM((8, width), F32),
+            pltpu.VMEM((24, width), F32),
             pltpu.VMEM((8, count), F32),
             pltpu.VMEM((total, 128), BF16),
             pltpu.VMEM((K_DIST, count), BF16),
@@ -220,30 +219,41 @@
     return lax.ppermute(array, AXES, [(i, i ^ mask) for i in range(devices)])
 
 
-def visitors(home, devices):
+def near_blocks(home, devices):
     levels = devices.bit_length() - 1
-    near = [flip(home, 1 << bit, devices) for bit in range(levels)]
+    return [flip(home, 1 << bit, devices) for bit in range(levels)]
+
+
+def far_stacks(near):
+    levels = len(near)
     order = [bit for bit in (0, 1, 2, 4, 3, 5, 6) if bit < levels]
     order += [bit for bit in range(levels) if bit not in order]
-    got, masks = [], []
+    stacks, lasts, masks = [], [], []
     for place, last in enumerate(order[:-1]):
         others = order[place + 1 :]
-        got.append(flip(jnp.stack([near[bit] for bit in others]), 1 << last, devices))
+        stacks.append(jnp.stack([near[bit] for bit in others]))
+        lasts.append(1 << last)
         masks += [1 << last | 1 << bit for bit in others]
-    return jnp.concatenate(got, 0), masks
+    return stacks, lasts, masks
 
 
 def body(positions, strengths, plan):
     devices = lax.axis_size(AXES)
     home = jnp.concatenate([positions, strengths], 0)
-    blocks, masks = visitors(home, devices)
+    half = home.shape[1] // 2
+    near = near_blocks(home, devices)
+    zero = jnp.zeros((1,), jnp.int32)
+    partial, _ = pair_sums(zero, home[None, :, :half], home, jnp.zeros_like(home), 512)
+    stacks, lasts, masks = far_stacks(near)
     own_masks = jnp.bitwise_xor(plan[:, 0], lax.axis_index(AXES).astype(jnp.int32))
     hits = own_masks[:, None] == jnp.asarray(masks, jnp.int32)[None, :]
     picks = jnp.sum(jnp.where(hits, jnp.arange(len(masks), dtype=jnp.int32)[None, :], 0), 1)
-    nothing = jnp.zeros_like(home)
-    partial, _ = pair_sums(jnp.zeros((1,), jnp.int32), home[None], home, nothing)
-    totals, peaks = pair_sums(picks.astype(jnp.int32), blocks, home, partial)
-    peak_sq = lax.pmax(peaks[0, 0], AXES)
+    partial, stacks = lax.optimization_barrier((partial, stacks))
+    far = [flip(stack, last, devices) for stack, last in zip(stacks, lasts)]
+    partial, _ = pair_sums(zero, home[None, :, half:], home, partial, 512)
+    totals, peaks = pair_sums(picks.astype(jnp.int32), jnp.concatenate(far, 0), home, partial)
+    every = lax.all_to_all(peaks[0:devices], AXES, 0, 0, tiled=True)
+    peak_sq = jnp.max(every)
     stretch = totals[3:]
     new_strengths = strengths + STEP_RATE / (jnp.sqrt(peak_sq) + 1e-06) * stretch
     return (totals[:3], new_strengths)

time: 328 us -> 264 us (0.80)
  blocking collectives: 65.9 us -> 18.8 us
  Pallas kernels: 218 us -> 205 us
  waiting for transfers between devices: 16.1 us -> 12.7 us
    pmax x1 -> x0, blocking collectives: 65.9 us -> none  [body(): peak_sq = lax.pmax(peaks[0, 0], AXES)]
    all_to_all x0 -> x1, blocking collectives: none -> 18.8 us  [body(): every = lax.all_to_all(peaks[0:devices], AXES, 0, 0, tiled=True)]
    pallas_call x2 -> x3, Pallas kernels: 218 us -> 205 us  [pair_sums(): pl.pallas_call(functools.partial(pair_kernel, slots, chunk_size), out_sha...]
    ppermute x12, waiting for transfers between devices: 16.1 us -> 12.7 us  [flip(): return lax.ppermute(array, AXES, [(i, i ^ mask) for i in range(devices)])]
  transfers between devices with their start and end apart: 12 -> 12, of which waited for: 4 -> 2; matrix products, arithmetic and copies ran while one was open for 1% -> 1% of each run, Pallas kernels for 8% -> 10%
where the time goes in v2:
time: 264 us
  Pallas kernels  205 us (78%)
  blocking collectives  18.8 us (7%)
  starting transfers between devices  17.9 us (7%)
  waiting for transfers between devices  12.7 us (5%)
  other arithmetic  5.46 us (2%)
    pallas_call x3, Pallas kernels, pair_sums(): pl.pallas_call(functools.partial(pair_kernel, slots, chunk_size), out_sha...  205 us
    all_to_all x1, blocking collectives, body(): every = lax.all_to_all(peaks[0:devices], AXES, 0, 0, tiled=True)  18.8 us
    ppermute x12, starting transfers between devices, flip(): return lax.ppermute(array, AXES, [(i, i ^ mask) for i in range(devices)])  17.9 us
    ppermute x12, waiting for transfers between devices, flip(): return lax.ppermute(array, AXES, [(i, i ^ mask) for i in range(devices)])  12.7 us
  transfers between devices with their start and end apart: 12, of which 2 were waited for; matrix products, arithmetic and copies ran while one was open for 1% of the time, Pallas kernels for 10%

profile of v2, /device:TPU:1, one launch (start us, length us, event | category | flops | bytes accessed | tf_op | source)
XLA Modules:
  0.0 263.9 jit_solution(10806280444984158739)
XLA Ops:
  0.6 0.0 copy-start.3
  0.6 0.9 pad_maximum_fusion.3.home_ref
  1.5 0.0 copy-start.1
  1.5 0.0 copy-start.4
  1.5 3.8 %collective-permute-start.5 = (f32[6,3072]{1,0:T(8,128)S(1)}, f32[6,3072]{1,0:T(8,128)S(1)}, u32[]{:S(2)}, u32[]{:S(2)}) collective-permute-start(f32[6,3072]{1,0:T(8,128)S(1)} %pad_maximum_fusion.3.home_ref), channel_id=1, source_target_pairs={{0,64},{1,65},{2,66},{3,67},{4,68},{5,69},{6,70},{7,71},{8,72},{9,... | collective-permute-start | bytes 221192 | tf_op jit(solution)/shard_map/ppermute | solution.py:219
  5.3 3.6 %collective-permute-start.4 = (f32[6,3072]{1,0:T(8,128)S(1)}, f32[6,3072]{1,0:T(8,128)S(1)}, u32[]{:S(2)}, u32[]{:S(2)}) collective-permute-start(f32[6,3072]{1,0:T(8,128)S(1)} %pad_maximum_fusion.3.home_ref), channel_id=1, source_target_pairs={{0,32},{1,33},{2,34},{3,35},{4,36},{5,37},{6,38},{7,39},{8,40},{9,... | collective-permute-start | bytes 221192 | tf_op jit(solution)/shard_map/ppermute | solution.py:219
  8.9 2.7 %collective-permute-start.3 = (f32[6,3072]{1,0:T(8,128)S(1)}, f32[6,3072]{1,0:T(8,128)S(1)}, u32[]{:S(2)}, u32[]{:S(2)}) collective-permute-start(f32[6,3072]{1,0:T(8,128)S(1)} %pad_maximum_fusion.3.home_ref), channel_id=1, source_target_pairs={{0,8},{1,9},{2,10},{3,11},{4,12},{5,13},{6,14},{7,15},{8,0},{9,1},... | collective-permute-start | bytes 221192 | tf_op jit(solution)/shard_map/ppermute | solution.py:219
  11.7 0.7 collective-permute-start.2
  12.4 0.3 collective-permute-start.1
  12.7 1.4 fusion.3
  14.2 0.6 broadcast_in_dim.27.carry_ref
  14.8 0.0 copy-done.1
  14.8 13.6 %shard_map.59 = (f32[6,3072]{1,0:T(8,128)}, f32[128,128]{1,0:T(8,128)}) custom-call(s32[1]{0:T(128)} %constant.9.clone.1.pick_ref, f32[1,6,1536]{2,1,0:T(8,128)} %get-tuple-element.27.src_ref, f32[6,3072]{1,0:T(8,128)} %copy-done.1, f32[6,3072]{1,0:T(8,128)} %broadcast_in_dim.27.carry_ref), custom_call_target="tpu_custom_call" | custom-call | tf_op jit(solution)/shard_map/pallas_call | solution.py:194
  28.4 0.0 collective-permute-done.5
  28.5 0.4 collective-permute-start
  28.9 0.0 collective-permute-done.4
  28.9 0.0 collective-permute-done.3
  28.9 0.0 collective-permute-done.2
  29.0 3.2 %collective-permute-done = f32[6,3072]{1,0:T(8,128)S(1)} collective-permute-done((f32[6,3072]{1,0:T(8,128)}, f32[6,3072]{1,0:T(8,128)S(1)}, u32[]{:S(2)}, u32[]{:S(2)}) %collective-permute-start) | collective-permute-done | bytes 73760 | tf_op jit(solution)/shard_map/ppermute | solution.py:219
  32.2 0.0 collective-permute-done.1
  32.3 3.3 %collective-permute-start.6 = (f32[6,6,3072]{2,1,0:T(8,128)S(1)}, f32[6,6,3072]{2,1,0:T(8,128)S(1)}, u32[]{:S(2)}, u32[]{:S(2)}) collective-permute-start(f32[6,6,3072]{2,1,0:T(8,128)S(1)} %get-tuple-element.14), channel_id=1, source_target_pairs={{0,1},{1,0},{2,3},{3,2},{4,5},{5,4},{6,7},{7,6},{8,9},{9,8},{10,11... | collective-permute-start | bytes 1327112 | tf_op jit(solution)/shard_map/ppermute | solution.py:219
  35.6 0.0 copy-done.3
  35.6 0.4 collective-permute-start.7
  36.0 0.0 copy-done.4
  36.0 0.7 select_reduce_fusion.pick_ref
  36.7 0.8 collective-permute-start.11
  37.6 1.7 collective-permute-start.10
  39.3 0.0 collective-permute-start.9
  39.3 13.6 %shard_map.60 = (f32[6,3072]{1,0:T(8,128)}, f32[128,128]{1,0:T(8,128)}) custom-call(s32[1]{0:T(128)} %constant.9.clone.1.pick_ref, f32[1,6,1536]{2,1,0:T(8,128)} %get-tuple-element.26.src_ref, f32[6,3072]{1,0:T(8,128)} %copy-done.1, f32[6,3072]{1,0:T(8,128)} %get-tuple-element.20.carry_ref), custom_call_target="tpu_custom_call" | custom-call | tf_op jit(solution)/shard_map/pallas_call | solution.py:194
  52.9 0.0 collective-permute-done.6
  52.9 0.0 collective-permute-start.8
  53.0 0.0 collective-permute-done.7
  53.0 0.0 copy-start.2
  53.1 9.5 %collective-permute-done.8 = f32[4,6,3072]{2,1,0:T(8,128)S(1)} collective-permute-done((f32[4,6,3072]{2,1,0:T(8,128)S(1)}, f32[4,6,3072]{2,1,0:T(8,128)S(1)}, u32[]{:S(2)}, u32[]{:S(2)}) %collective-permute-start.8) | collective-permute-done | bytes 294944 | tf_op jit(solution)/shard_map/ppermute | solution.py:219
  62.6 0.0 collective-permute-done.9
  62.6 0.0 collective-permute-done.10
  62.7 0.0 collective-permute-done.11
  62.7 0.0 copy-start
  62.7 1.3 copy-done
  64.0 177.9 %shard_map.61 = (f32[6,3072]{1,0:T(8,128)}, f32[128,128]{1,0:T(8,128)}) custom-call(s32[8]{0:T(128)} %select_reduce_fusion.pick_ref, f32[21,6,3072]{2,1,0:T(8,128)} %copy-done, f32[6,3072]{1,0:T(8,128)} %copy-done.1, f32[6,3072]{1,0:T(8,128)} %get-tuple-element.21.carry_ref), custom_call_target="tpu_custom_call" | custom-call | tf_op jit(solution)/shard_map/pallas_call | solution.py:194
  241.9 18.8 %all_to_all.9 = f32[128,1,128]{2,1,0:T(1,128)S(1)} all-to-all(f32[128,1,128]{2,1,0:T(1,128)} %bitcast.36), channel_id=1, replica_groups=mesh['grp'=2,'dev'=64] {'grp','dev'}, dimensions={0} | all-to-all | bytes 131072 | tf_op jit(solution)/shard_map/all_to_all | solution.py:255
  260.7 0.7 reduce_max.9
  262.2 0.0 copy-done.2
  262.2 1.6 multiply_add_fusion
  (16 shorter events, 0.3 us)
Async XLA Ops:
  0.6 35.0 %copy-start.3 = (s32[8,1]{0,1:T(1,128)S(1)}, s32[8,1]{0,1:T(1,128)}, u32[]{:S(2)}) copy-start(s32[8,1]{0,1:T(1,128)} %param.6) | copy-start | bytes 100
  1.5 13.3 %copy-start.1 = (f32[6,3072]{1,0:T(8,128)}, f32[6,3072]{1,0:T(8,128)S(1)}, u32[]{:S(2)}) copy-start(f32[6,3072]{1,0:T(8,128)S(1)} %pad_maximum_fusion.3.home_ref) | copy-start | bytes 221188
  1.5 34.5 %copy-start.4 = (s32[21]{0:T(128)S(1)}, s32[21]{0:T(128)}, u32[]{:S(2)}) copy-start(s32[21]{0:T(128)} %constant.25.clone) | copy-start | bytes 256
  1.5 26.9 %collective-permute-start.5 = (f32[6,3072]{1,0:T(8,128)S(1)}, f32[6,3072]{1,0:T(8,128)S(1)}, u32[]{:S(2)}, u32[]{:S(2)}) collective-permute-start(f32[6,3072]{1,0:T(8,128)S(1)} %pad_maximum_fusion.3.home_ref), channel_id=1, source_target_pairs={{0,64},{1,65},{2,66},{3,67},{4,68},{5,69},{6,70},{7,71},{8,72},{9,... | collective-permute-start | bytes 221192 | tf_op jit(solution)/shard_map/ppermute | solution.py:219
  5.3 23.5 %collective-permute-start.4 = (f32[6,3072]{1,0:T(8,128)S(1)}, f32[6,3072]{1,0:T(8,128)S(1)}, u32[]{:S(2)}, u32[]{:S(2)}) collective-permute-start(f32[6,3072]{1,0:T(8,128)S(1)} %pad_maximum_fusion.3.home_ref), channel_id=1, source_target_pairs={{0,32},{1,33},{2,34},{3,35},{4,36},{5,37},{6,38},{7,39},{8,40},{9,... | collective-permute-start | bytes 221192 | tf_op jit(solution)/shard_map/ppermute | solution.py:219
  8.9 19.9 %collective-permute-start.3 = (f32[6,3072]{1,0:T(8,128)S(1)}, f32[6,3072]{1,0:T(8,128)S(1)}, u32[]{:S(2)}, u32[]{:S(2)}) collective-permute-start(f32[6,3072]{1,0:T(8,128)S(1)} %pad_maximum_fusion.3.home_ref), channel_id=1, source_target_pairs={{0,8},{1,9},{2,10},{3,11},{4,12},{5,13},{6,14},{7,15},{8,0},{9,1},... | collective-permute-start | bytes 221192 | tf_op jit(solution)/shard_map/ppermute | solution.py:219
  11.7 17.2 %collective-permute-start.2 = (f32[6,3072]{1,0:T(8,128)S(1)}, f32[6,3072]{1,0:T(8,128)S(1)}, u32[]{:S(2)}, u32[]{:S(2)}) collective-permute-start(f32[6,3072]{1,0:T(8,128)S(1)} %pad_maximum_fusion.3.home_ref), channel_id=1, source_target_pairs={{0,16},{1,17},{2,18},{3,19},{4,20},{5,21},{6,22},{7,23},{8,24},{9,... | collective-permute-start | bytes 221192 | tf_op jit(solution)/shard_map/ppermute | solution.py:219
  12.4 19.8 %collective-permute-start.1 = (f32[6,3072]{1,0:T(8,128)S(1)}, f32[6,3072]{1,0:T(8,128)S(1)}, u32[]{:S(2)}, u32[]{:S(2)}) collective-permute-start(f32[6,3072]{1,0:T(8,128)S(1)} %pad_maximum_fusion.3.home_ref), channel_id=1, source_target_pairs={{0,4},{1,5},{2,6},{3,7},{4,0},{5,1},{6,2},{7,3},{8,12},{9,13},{10,... | collective-permute-start | bytes 221192 | tf_op jit(solution)/shard_map/ppermute | solution.py:219
  28.5 3.7 %collective-permute-start = (f32[6,3072]{1,0:T(8,128)}, f32[6,3072]{1,0:T(8,128)S(1)}, u32[]{:S(2)}, u32[]{:S(2)}) collective-permute-start(f32[6,3072]{1,0:T(8,128)} %copy-done.1), channel_id=1, source_target_pairs={{0,2},{1,3},{2,0},{3,1},{4,6},{5,7},{6,4},{7,5},{8,10},{9,11},{10,... | collective-permute-start | bytes 221192 | tf_op jit(solution)/shard_map/ppermute | solution.py:219
  32.3 20.6 %collective-permute-start.6 = (f32[6,6,3072]{2,1,0:T(8,128)S(1)}, f32[6,6,3072]{2,1,0:T(8,128)S(1)}, u32[]{:S(2)}, u32[]{:S(2)}) collective-permute-start(f32[6,6,3072]{2,1,0:T(8,128)S(1)} %get-tuple-element.14), channel_id=1, source_target_pairs={{0,1},{1,0},{2,3},{3,2},{4,5},{5,4},{6,7},{7,6},{8,9},{9,8},{10,11... | collective-permute-start | bytes 1327112 | tf_op jit(solution)/shard_map/ppermute | solution.py:219
  35.6 17.4 %collective-permute-start.7 = (f32[5,6,3072]{2,1,0:T(8,128)S(1)}, f32[5,6,3072]{2,1,0:T(8,128)S(1)}, u32[]{:S(2)}, u32[]{:S(2)}) collective-permute-start(f32[5,6,3072]{2,1,0:T(8,128)S(1)} %get-tuple-element.15), channel_id=1, source_target_pairs={{0,2},{1,3},{2,0},{3,1},{4,6},{5,7},{6,4},{7,5},{8,10},{9,11},{10,... | collective-permute-start | bytes 1105928 | tf_op jit(solution)/shard_map/ppermute | solution.py:219
  36.7 25.9 %collective-permute-start.11 = (f32[1,6,3072]{2,1,0:T(8,128)S(1)}, f32[1,6,3072]{2,1,0:T(8,128)S(1)}, u32[]{:S(2)}, u32[]{:S(2)}) collective-permute-start(f32[1,6,3072]{2,1,0:T(8,128)S(1)} %bitcast.29), channel_id=1, source_target_pairs={{0,32},{1,33},{2,34},{3,35},{4,36},{5,37},{6,38},{7,39},{8,40},{9,... | collective-permute-start | bytes 221192 | tf_op jit(solution)/shard_map/ppermute | solution.py:219
  37.6 25.1 %collective-permute-start.10 = (f32[2,6,3072]{2,1,0:T(8,128)S(1)}, f32[2,6,3072]{2,1,0:T(8,128)S(1)}, u32[]{:S(2)}, u32[]{:S(2)}) collective-permute-start(f32[2,6,3072]{2,1,0:T(8,128)S(1)} %pad_maximum_fusion.2), channel_id=1, source_target_pairs={{0,8},{1,9},{2,10},{3,11},{4,12},{5,13},{6,14},{7,15},{8,0},{9,1},... | collective-permute-start | bytes 442376 | tf_op jit(solution)/shard_map/ppermute | solution.py:219
  39.3 23.3 %collective-permute-start.9 = (f32[3,6,3072]{2,1,0:T(8,128)S(1)}, f32[3,6,3072]{2,1,0:T(8,128)S(1)}, u32[]{:S(2)}, u32[]{:S(2)}) collective-permute-start(f32[3,6,3072]{2,1,0:T(8,128)S(1)} %pad_maximum_fusion.1), channel_id=1, source_target_pairs={{0,16},{1,17},{2,18},{3,19},{4,20},{5,21},{6,22},{7,23},{8,24},{9,... | collective-permute-start | bytes 663560 | tf_op jit(solution)/shard_map/ppermute | solution.py:219
  52.9 9.6 %collective-permute-start.8 = (f32[4,6,3072]{2,1,0:T(8,128)S(1)}, f32[4,6,3072]{2,1,0:T(8,128)S(1)}, u32[]{:S(2)}, u32[]{:S(2)}) collective-permute-start(f32[4,6,3072]{2,1,0:T(8,128)S(1)} %pad_maximum_fusion), channel_id=1, source_target_pairs={{0,4},{1,5},{2,6},{3,7},{4,0},{5,1},{6,2},{7,3},{8,12},{9,13},{10,... | collective-permute-start | bytes 884744 | tf_op jit(solution)/shard_map/ppermute | solution.py:219
  53.0 209.2 %copy-start.2 = (f32[3,3072]{1,0:T(4,128)S(1)}, f32[3,3072]{1,0:T(4,128)}, u32[]{:S(2)}) copy-start(f32[3,3072]{1,0:T(4,128)} %param.5) | copy-start | bytes 110596
  62.7 1.3 copy-start

commit v3 on v2

--- a/solution.py
+++ b/solution.py
@@ -16,8 +16,8 @@
 PIECE = 64
 LANES = 256
 K_DIST = 48
-ROWS3 = 16
-ROWS5 = 80
+ROWS3 = 32
+ROWS5 = 64
 BF16 = jnp.bfloat16
 F32 = jnp.float32
 
@@ -49,7 +49,7 @@
 
 def pair_kernel(
     slots, chunk_size, pick_ref, src_ref, home_ref, carry_ref, out_ref, peak_ref,
-    feat3, feat5, dist8, fs, ft, x3, x5, o3, o5, *bufs
+    feat3, feat5, stack5, dist8, fs, ft, x3, x5, o3, o5, *bufs
 ):
     count = home_ref.shape[1]
     width = src_ref.shape[2]
@@ -63,6 +63,7 @@
     scale = jnp.maximum(largest, 1e-30)
 
     feat3[...] = jnp.zeros_like(feat3)
+    stack5[...] = jnp.zeros_like(stack5)
     dist8[...] = jnp.zeros_like(dist8)
 
     def fill(slot, _):
@@ -76,9 +77,10 @@
             feat3[3 + k : 4 + k, :] = moment[k]
             feat5[k : k + 1, :] = strength[k]
             feat5[3 + k : 4 + k, :] = moment[k]
-            for l in range(3):
-                feat5[6 + 3 * k + l : 7 + 3 * k + l, :] = pos[k] * strength[l]
-                feat5[15 + 3 * k + l : 16 + 3 * k + l, :] = pos[k] * moment[l]
+            feat5[6 + k : 7 + k, :] = pos[k] * strength[k]
+            feat5[9 + k : 10 + k, :] = pos[k] * strength[(k + 1) % 3]
+            for l in range(3 if k < 2 else 2):
+                feat5[12 + 3 * k + l : 13 + 3 * k + l, :] = pos[k] * moment[l]
             dist8[k : k + 1, 0:width] = pos[k]
         dist8[3:4, 0:width] = pos[0] * pos[0] + pos[1] * pos[1] + pos[2] * pos[2]
         dist8[4:5, 0:width] = jnp.ones_like(pos[0])
@@ -88,9 +90,11 @@
         fs[cols, :] = rows.T.astype(BF16)
         f3 = feat3[...]
         f5 = feat5[...]
-        x3[:, cols] = jnp.concatenate(pieces(f3, BF16, 2), 0).astype(BF16)
-        p = pieces(f5, BF16, 3)
-        x5[:, cols] = jnp.concatenate(p + [jnp.zeros_like(f3)], 0).astype(BF16)
+        p = pieces(f3, BF16, 3)
+        x3[:, cols] = jnp.concatenate(p + [jnp.zeros_like(f3)], 0).astype(BF16)
+        for number, part in enumerate(pieces(f5, BF16, 3)):
+            stack5[20 * number : 20 * number + 20, :] = part
+        x5[:, cols] = stack5[...].astype(BF16)
         return 0
 
     lax.fori_loop(0, slots, fill, 0)
@@ -156,8 +160,8 @@
 
     lax.fori_loop(0, tiles * chunks // 2, two_steps, 0)
 
-    sum3 = o3[0:8, :] + o3[8:16, :]
-    sum5 = o5[0:24, :] + o5[24:48, :] + o5[48:72, :]
+    sum3 = o3[0:8, :] + o3[8:16, :] + o3[16:24, :]
+    sum5 = o5[0:20, :] + o5[20:40, :] + o5[40:60, :]
     factor = -INV_FOUR_PI * scale
     own = [home_ref[3 + k : 4 + k, :] for k in range(3)]
     spin = rows_of(sum3[0:3])
@@ -166,12 +170,22 @@
     moment5 = rows_of(sum5[3:6])
     along = own[0] * pos[0] + own[1] * pos[1] + own[2] * pos[2]
     swirl, lever = [], []
+    cross = [[None] * 3 for _ in range(3)]
+    arm = [[None] * 3 for _ in range(3)]
+    for k in range(3):
+        after = (k + 1) % 3
+        cross[k][k] = sum5[6 + k : 7 + k, :]
+        cross[k][after] = sum5[9 + k : 10 + k, :]
+        cross[after][k] = cross[k][after] - moment5[(k + 2) % 3]
+        for l in range(3 if k < 2 else 2):
+            arm[k][l] = sum5[12 + 3 * k + l : 13 + 3 * k + l, :]
+    arm[2][2] = -(arm[0][0] + arm[1][1])
     for l in range(3):
         total = along * plain5[l]
         other = along * moment5[l]
         for k in range(3):
-            total -= own[k] * sum5[6 + 3 * k + l : 7 + 3 * k + l, :]
-            other -= own[k] * sum5[15 + 3 * k + l : 16 + 3 * k + l, :]
+            total -= own[k] * cross[k][l]
+            other -= own[k] * arm[k][l]
         swirl.append(total)
         lever.append(other)
     twist = cross_rows(pos, swirl)
@@ -201,7 +215,8 @@
         out_specs=(vmem, vmem),
         scratch_shapes=[
             pltpu.VMEM((8, width), F32),
-            pltpu.VMEM((24, width), F32),
+            pltpu.VMEM((20, width), F32),
+            pltpu.VMEM((ROWS5, width), F32),
             pltpu.VMEM((8, count), F32),
             pltpu.VMEM((total, 128), BF16),
             pltpu.VMEM((K_DIST, count), BF16),
@@ -240,17 +255,17 @@
 def body(positions, strengths, plan):
     devices = lax.axis_size(AXES)
     home = jnp.concatenate([positions, strengths], 0)
-    half = home.shape[1] // 2
+    third = home.shape[1] // 3
     near = near_blocks(home, devices)
     zero = jnp.zeros((1,), jnp.int32)
-    partial, _ = pair_sums(zero, home[None, :, :half], home, jnp.zeros_like(home), 512)
+    partial, _ = pair_sums(zero, home[None, :, :third], home, jnp.zeros_like(home), 512)
     stacks, lasts, masks = far_stacks(near)
     own_masks = jnp.bitwise_xor(plan[:, 0], lax.axis_index(AXES).astype(jnp.int32))
     hits = own_masks[:, None] == jnp.asarray(masks, jnp.int32)[None, :]
     picks = jnp.sum(jnp.where(hits, jnp.arange(len(masks), dtype=jnp.int32)[None, :], 0), 1)
     partial, stacks = lax.optimization_barrier((partial, stacks))
     far = [flip(stack, last, devices) for stack, last in zip(stacks, lasts)]
-    partial, _ = pair_sums(zero, home[None, :, half:], home, partial, 512)
+    partial, _ = pair_sums(zero, home[None, :, third:], home, partial, 512)
     totals, peaks = pair_sums(picks.astype(jnp.int32), jnp.concatenate(far, 0), home, partial)
     every = lax.all_to_all(peaks[0:devices], AXES, 0, 0, tiled=True)
     peak_sq = jnp.max(every)

time: 264 us -> 253 us (0.958)
  Pallas kernels: 205 us -> 200 us
  waiting for transfers between devices: 12.7 us -> 7.89 us
    pallas_call x3, Pallas kernels: 205 us -> 200 us  [pair_sums(): pl.pallas_call(functools.partial(pair_kernel, slots, chunk_size), out_sha...]
    ppermute x12, waiting for transfers between devices: 12.7 us -> 7.89 us  [flip(): return lax.ppermute(array, AXES, [(i, i ^ mask) for i in range(devices)])]
  transfers between devices with their start and end apart: 12 -> 12, of which waited for: 2 -> 2; matrix products, arithmetic and copies ran while one was open for 1% -> 1% of each run, Pallas kernels for 10% -> 11%
where the time goes in v3:
time: 253 us
  Pallas kernels  200 us (79%)
  starting transfers between devices  18.3 us (7%)
  blocking collectives  17.2 us (7%)
  waiting for transfers between devices  7.89 us (3%)
  other arithmetic  6.03 us (2%)
    pallas_call x3, Pallas kernels, pair_sums(): pl.pallas_call(functools.partial(pair_kernel, slots, chunk_size), out_sha...  200 us
    ppermute x12, starting transfers between devices, flip(): return lax.ppermute(array, AXES, [(i, i ^ mask) for i in range(devices)])  18.3 us
    all_to_all x1, blocking collectives, body(): every = lax.all_to_all(peaks[0:devices], AXES, 0, 0, tiled=True)  17.2 us
    ppermute x12, waiting for transfers between devices, flip(): return lax.ppermute(array, AXES, [(i, i ^ mask) for i in range(devices)])  7.89 us
  transfers between devices with their start and end apart: 12, of which 2 were waited for; matrix products, arithmetic and copies ran while one was open for 1% of the time, Pallas kernels for 11%

profile of v3, /device:TPU:1, one launch (start us, length us, event | category | flops | bytes accessed | tf_op | source)
XLA Modules:
  0.0 253.0 jit_solution(687865165739122421)
XLA Ops:
  0.6 0.0 copy-start.3
  0.6 0.0 copy-start.2
  0.7 0.0 copy-start.4
  0.7 0.9 pad_maximum_fusion.3.home_ref
  1.5 0.0 copy-start.1
  1.6 0.0 copy-start.5
  1.6 2.2 collective-permute-start
  3.8 1.6 collective-permute-start.2
  5.4 2.7 %collective-permute-start.3 = (f32[6,3072]{1,0:T(8,128)S(1)}, f32[6,3072]{1,0:T(8,128)S(1)}, u32[]{:S(2)}, u32[]{:S(2)}) collective-permute-start(f32[6,3072]{1,0:T(8,128)S(1)} %pad_maximum_fusion.3.home_ref), channel_id=1, source_target_pairs={{0,8},{1,9},{2,10},{3,11},{4,12},{5,13},{6,14},{7,15},{8,0},{9,1},... | collective-permute-start | bytes 221192 | tf_op jit(solution)/shard_map/ppermute | solution.py:234
  8.2 3.3 %collective-permute-start.4 = (f32[6,3072]{1,0:T(8,128)S(1)}, f32[6,3072]{1,0:T(8,128)S(1)}, u32[]{:S(2)}, u32[]{:S(2)}) collective-permute-start(f32[6,3072]{1,0:T(8,128)S(1)} %pad_maximum_fusion.3.home_ref), channel_id=1, source_target_pairs={{0,32},{1,33},{2,34},{3,35},{4,36},{5,37},{6,38},{7,39},{8,40},{9,... | collective-permute-start | bytes 221192 | tf_op jit(solution)/shard_map/ppermute | solution.py:234
  11.5 2.6 %collective-permute-start.5 = (f32[6,3072]{1,0:T(8,128)S(1)}, f32[6,3072]{1,0:T(8,128)S(1)}, u32[]{:S(2)}, u32[]{:S(2)}) collective-permute-start(f32[6,3072]{1,0:T(8,128)S(1)} %pad_maximum_fusion.3.home_ref), channel_id=1, source_target_pairs={{0,64},{1,65},{2,66},{3,67},{4,68},{5,69},{6,70},{7,71},{8,72},{9,... | collective-permute-start | bytes 221192 | tf_op jit(solution)/shard_map/ppermute | solution.py:234
  14.1 1.4 fusion.3.src_ref
  15.4 0.6 broadcast_in_dim.27.carry_ref
  16.1 0.0 copy-done.1
  16.1 10.1 %shard_map.59 = (f32[6,3072]{1,0:T(8,128)}, f32[128,128]{1,0:T(8,128)}) custom-call(s32[1]{0:T(128)} %constant.9.clone.1.pick_ref, f32[1,6,1024]{2,1,0:T(8,128)} %fusion.3.src_ref, f32[6,3072]{1,0:T(8,128)} %copy-done.1, f32[6,3072]{1,0:T(8,128)} %broadcast_in_dim.27.carry_ref), custom_call_target="tpu_custom_call" | custom-call | tf_op jit(solution)/shard_map/pallas_call | solution.py:208
  26.2 0.0 collective-permute-done.2
  26.2 0.3 collective-permute-start.1
  26.5 0.0 collective-permute-done.3
  26.5 0.0 collective-permute-done.4
  26.5 0.0 collective-permute-done.5
  26.6 0.0 collective-permute-done
  26.6 3.2 %collective-permute-done.1 = f32[6,3072]{1,0:T(8,128)S(1)} collective-permute-done((f32[6,3072]{1,0:T(8,128)}, f32[6,3072]{1,0:T(8,128)S(1)}, u32[]{:S(2)}, u32[]{:S(2)}) %collective-permute-start.1) | collective-permute-done | bytes 73760 | tf_op jit(solution)/shard_map/ppermute | solution.py:234
  29.9 3.3 %collective-permute-start.6 = (f32[6,6,3072]{2,1,0:T(8,128)S(1)}, f32[6,6,3072]{2,1,0:T(8,128)S(1)}, u32[]{:S(2)}, u32[]{:S(2)}) collective-permute-start(f32[6,6,3072]{2,1,0:T(8,128)S(1)} %get-tuple-element.14), channel_id=1, source_target_pairs={{0,1},{1,0},{2,3},{3,2},{4,5},{5,4},{6,7},{7,6},{8,9},{9,8},{10,11... | collective-permute-start | bytes 1327112 | tf_op jit(solution)/shard_map/ppermute | solution.py:234
  33.3 0.0 copy-done.4
  33.3 0.0 copy-done.3
  33.3 0.0 copy-done.2
  33.3 0.6 fusion.1.src_ref
  33.9 0.0 collective-permute-start.7
  33.9 0.0 copy-done.5
  33.9 0.7 select_reduce_fusion.pick_ref
  34.6 0.3 collective-permute-start.8
  34.9 0.0 collective-permute-start.9
  34.9 1.7 collective-permute-start.10
  36.6 17.6 %shard_map.60 = (f32[6,3072]{1,0:T(8,128)}, f32[128,128]{1,0:T(8,128)}) custom-call(s32[1]{0:T(128)} %constant.9.clone.1.pick_ref, f32[1,6,2048]{2,1,0:T(8,128)} %fusion.1.src_ref, f32[6,3072]{1,0:T(8,128)} %copy-done.1, f32[6,3072]{1,0:T(8,128)} %get-tuple-element.20.carry_ref), custom_call_target="tpu_custom_call" | custom-call | tf_op jit(solution)/shard_map/pallas_call | solution.py:208
  54.3 0.0 collective-permute-done.6
  54.3 0.1 collective-permute-start.11
  54.4 0.0 collective-permute-done.7
  54.5 0.0 collective-permute-done.8
  54.5 0.0 collective-permute-done.9
  54.6 0.0 collective-permute-done.10
  54.6 4.7 %collective-permute-done.11 = f32[1,6,3072]{2,1,0:T(8,128)S(1)} collective-permute-done((f32[1,6,3072]{2,1,0:T(8,128)S(1)}, f32[1,6,3072]{2,1,0:T(8,128)S(1)}, u32[]{:S(2)}, u32[]{:S(2)}) %collective-permute-start.11) | collective-permute-done | bytes 73760 | tf_op jit(solution)/shard_map/ppermute | solution.py:234
  59.3 0.0 copy-start
  59.3 1.3 copy-done
  60.6 172.1 %shard_map.61 = (f32[6,3072]{1,0:T(8,128)}, f32[128,128]{1,0:T(8,128)}) custom-call(s32[8]{0:T(128)} %select_reduce_fusion.pick_ref, f32[21,6,3072]{2,1,0:T(8,128)} %copy-done, f32[6,3072]{1,0:T(8,128)} %copy-done.1, f32[6,3072]{1,0:T(8,128)} %get-tuple-element.21.carry_ref), custom_call_target="tpu_custom_call" | custom-call | tf_op jit(solution)/shard_map/pallas_call | solution.py:208
  232.7 17.2 %all_to_all.9 = f32[128,1,128]{2,1,0:T(1,128)S(1)} all-to-all(f32[128,1,128]{2,1,0:T(1,128)} %bitcast.36), channel_id=1, replica_groups=mesh['grp'=2,'dev'=64] {'grp','dev'}, dimensions={0} | all-to-all | bytes 131072 | tf_op jit(solution)/shard_map/all_to_all | solution.py:270
  249.9 0.7 reduce_max.9
  251.4 1.6 multiply_add_fusion
  (16 shorter events, 0.3 us)
Async XLA Ops:
  0.6 32.6 %copy-start.3 = (f32[3,3072]{1,0:T(4,128)S(1)}, f32[3,3072]{1,0:T(4,128)}, u32[]{:S(2)}) copy-start(f32[3,3072]{1,0:T(4,128)} %param.4) | copy-start | bytes 110596
  0.6 32.6 %copy-start.2 = (f32[3,3072]{1,0:T(4,128)S(1)}, f32[3,3072]{1,0:T(4,128)}, u32[]{:S(2)}) copy-start(f32[3,3072]{1,0:T(4,128)} %param.5) | copy-start | bytes 110596
  0.7 32.6 %copy-start.4 = (s32[8,1]{0,1:T(1,128)S(1)}, s32[8,1]{0,1:T(1,128)}, u32[]{:S(2)}) copy-start(s32[8,1]{0,1:T(1,128)} %param.6) | copy-start | bytes 100
  1.5 14.5 %copy-start.1 = (f32[6,3072]{1,0:T(8,128)}, f32[6,3072]{1,0:T(8,128)S(1)}, u32[]{:S(2)}) copy-start(f32[6,3072]{1,0:T(8,128)S(1)} %pad_maximum_fusion.3.home_ref) | copy-start | bytes 221188
  1.6 32.4 %copy-start.5 = (s32[21]{0:T(128)S(1)}, s32[21]{0:T(128)}, u32[]{:S(2)}) copy-start(s32[21]{0:T(128)} %constant.25.clone) | copy-start | bytes 256
  1.6 25.0 %collective-permute-start = (f32[6,3072]{1,0:T(8,128)S(1)}, f32[6,3072]{1,0:T(8,128)S(1)}, u32[]{:S(2)}, u32[]{:S(2)}) collective-permute-start(f32[6,3072]{1,0:T(8,128)S(1)} %pad_maximum_fusion.3.home_ref), channel_id=1, source_target_pairs={{0,2},{1,3},{2,0},{3,1},{4,6},{5,7},{6,4},{7,5},{8,10},{9,11},{10,... | collective-permute-start | bytes 221192 | tf_op jit(solution)/shard_map/ppermute | solution.py:234
  3.8 22.4 %collective-permute-start.2 = (f32[6,3072]{1,0:T(8,128)S(1)}, f32[6,3072]{1,0:T(8,128)S(1)}, u32[]{:S(2)}, u32[]{:S(2)}) collective-permute-start(f32[6,3072]{1,0:T(8,128)S(1)} %pad_maximum_fusion.3.home_ref), channel_id=1, source_target_pairs={{0,16},{1,17},{2,18},{3,19},{4,20},{5,21},{6,22},{7,23},{8,24},{9,... | collective-permute-start | bytes 221192 | tf_op jit(solution)/shard_map/ppermute | solution.py:234
  5.4 21.1 %collective-permute-start.3 = (f32[6,3072]{1,0:T(8,128)S(1)}, f32[6,3072]{1,0:T(8,128)S(1)}, u32[]{:S(2)}, u32[]{:S(2)}) collective-permute-start(f32[6,3072]{1,0:T(8,128)S(1)} %pad_maximum_fusion.3.home_ref), channel_id=1, source_target_pairs={{0,8},{1,9},{2,10},{3,11},{4,12},{5,13},{6,14},{7,15},{8,0},{9,1},... | collective-permute-start | bytes 221192 | tf_op jit(solution)/shard_map/ppermute | solution.py:234
  8.2 18.3 %collective-permute-start.4 = (f32[6,3072]{1,0:T(8,128)S(1)}, f32[6,3072]{1,0:T(8,128)S(1)}, u32[]{:S(2)}, u32[]{:S(2)}) collective-permute-start(f32[6,3072]{1,0:T(8,128)S(1)} %pad_maximum_fusion.3.home_ref), channel_id=1, source_target_pairs={{0,32},{1,33},{2,34},{3,35},{4,36},{5,37},{6,38},{7,39},{8,40},{9,... | collective-permute-start | bytes 221192 | tf_op jit(solution)/shard_map/ppermute | solution.py:234
  11.5 15.0 %collective-permute-start.5 = (f32[6,3072]{1,0:T(8,128)S(1)}, f32[6,3072]{1,0:T(8,128)S(1)}, u32[]{:S(2)}, u32[]{:S(2)}) collective-permute-start(f32[6,3072]{1,0:T(8,128)S(1)} %pad_maximum_fusion.3.home_ref), channel_id=1, source_target_pairs={{0,64},{1,65},{2,66},{3,67},{4,68},{5,69},{6,70},{7,71},{8,72},{9,... | collective-permute-start | bytes 221192 | tf_op jit(solution)/shard_map/ppermute | solution.py:234
  26.2 3.7 %collective-permute-start.1 = (f32[6,3072]{1,0:T(8,128)}, f32[6,3072]{1,0:T(8,128)S(1)}, u32[]{:S(2)}, u32[]{:S(2)}) collective-permute-start(f32[6,3072]{1,0:T(8,128)} %copy-done.1), channel_id=1, source_target_pairs={{0,4},{1,5},{2,6},{3,7},{4,0},{5,1},{6,2},{7,3},{8,12},{9,13},{10,... | collective-permute-start | bytes 221192 | tf_op jit(solution)/shard_map/ppermute | solution.py:234
  29.9 24.3 %collective-permute-start.6 = (f32[6,6,3072]{2,1,0:T(8,128)S(1)}, f32[6,6,3072]{2,1,0:T(8,128)S(1)}, u32[]{:S(2)}, u32[]{:S(2)}) collective-permute-start(f32[6,6,3072]{2,1,0:T(8,128)S(1)} %get-tuple-element.14), channel_id=1, source_target_pairs={{0,1},{1,0},{2,3},{3,2},{4,5},{5,4},{6,7},{7,6},{8,9},{9,8},{10,11... | collective-permute-start | bytes 1327112 | tf_op jit(solution)/shard_map/ppermute | solution.py:234
  33.9 20.5 %collective-permute-start.7 = (f32[5,6,3072]{2,1,0:T(8,128)S(1)}, f32[5,6,3072]{2,1,0:T(8,128)S(1)}, u32[]{:S(2)}, u32[]{:S(2)}) collective-permute-start(f32[5,6,3072]{2,1,0:T(8,128)S(1)} %get-tuple-element.15), channel_id=1, source_target_pairs={{0,2},{1,3},{2,0},{3,1},{4,6},{5,7},{6,4},{7,5},{8,10},{9,11},{10,... | collective-permute-start | bytes 1105928 | tf_op jit(solution)/shard_map/ppermute | solution.py:234
  34.6 19.9 %collective-permute-start.8 = (f32[4,6,3072]{2,1,0:T(8,128)S(1)}, f32[4,6,3072]{2,1,0:T(8,128)S(1)}, u32[]{:S(2)}, u32[]{:S(2)}) collective-permute-start(f32[4,6,3072]{2,1,0:T(8,128)S(1)} %pad_maximum_fusion), channel_id=1, source_target_pairs={{0,4},{1,5},{2,6},{3,7},{4,0},{5,1},{6,2},{7,3},{8,12},{9,13},{10,... | collective-permute-start | bytes 884744 | tf_op jit(solution)/shard_map/ppermute | solution.py:234
  34.9 19.6 %collective-permute-start.9 = (f32[3,6,3072]{2,1,0:T(8,128)S(1)}, f32[3,6,3072]{2,1,0:T(8,128)S(1)}, u32[]{:S(2)}, u32[]{:S(2)}) collective-permute-start(f32[3,6,3072]{2,1,0:T(8,128)S(1)} %pad_maximum_fusion.1), channel_id=1, source_target_pairs={{0,16},{1,17},{2,18},{3,19},{4,20},{5,21},{6,22},{7,23},{8,24},{9,... | collective-permute-start | bytes 663560 | tf_op jit(solution)/shard_map/ppermute | solution.py:234
  34.9 19.7 %collective-permute-start.10 = (f32[2,6,3072]{2,1,0:T(8,128)S(1)}, f32[2,6,3072]{2,1,0:T(8,128)S(1)}, u32[]{:S(2)}, u32[]{:S(2)}) collective-permute-start(f32[2,6,3072]{2,1,0:T(8,128)S(1)} %pad_maximum_fusion.2), channel_id=1, source_target_pairs={{0,8},{1,9},{2,10},{3,11},{4,12},{5,13},{6,14},{7,15},{8,0},{9,1},... | collective-permute-start | bytes 442376 | tf_op jit(solution)/shard_map/ppermute | solution.py:234
  54.3 5.0 %collective-permute-start.11 = (f32[1,6,3072]{2,1,0:T(8,128)S(1)}, f32[1,6,3072]{2,1,0:T(8,128)S(1)}, u32[]{:S(2)}, u32[]{:S(2)}) collective-permute-start(f32[1,6,3072]{2,1,0:T(8,128)S(1)} %bitcast.29), channel_id=1, source_target_pairs={{0,32},{1,33},{2,34},{3,35},{4,36},{5,37},{6,38},{7,39},{8,40},{9,... | collective-permute-start | bytes 221192 | tf_op jit(solution)/shard_map/ppermute | solution.py:234
  59.3 1.3 copy-start
